TPU v7x, 32 devices: a whole 2x2x4 slice. The times are simulated.
32 devices in a mesh: ctx: 8 (over z, y), wa: 4 (over x, core).
Axes of the slice: x: 2, y: 2, z: 4, core: 2. Of those that a mesh axis runs over, the one named last changes fastest.
Arguments:
- layer_input: bfloat16 [4096, 1536], P('ctx'), may hold values from -6 to 6
- segment_ids: int32 [4096], P('ctx'), may hold values from 0 to 4, as said below
- expert_ids: int32 [4096, 2], P('ctx'), may hold values from 0 to 7, all different within a row; in each aligned block of 512 rows (0 to 511, 512 to 1023, ...) at most 256 rows name the same one
- norm_gain: float32 [1536], replicated, may hold values from 0.1 to 1.9
- query_weight: bfloat16 [1536, 1536], P(None, 'wa'), may hold values from -0.15625 to 0.15625
- key_weight: bfloat16 [1536, 512], P(None, 'wa'), may hold values from -0.15625 to 0.15625
- value_weight: bfloat16 [1536, 512], P(None, 'wa'), may hold values from -0.15625 to 0.15625
- output_weight: bfloat16 [1536, 1536], P('wa'), may hold values from -2.5 to 2.5
- ffn_gain: float32 [1536], replicated, may hold values from 0.1 to 1.9
- router_weight: bfloat16 [1536, 8], replicated, may hold values from -0.078125 to 0.078125
- gate_weight: bfloat16 [8, 1536, 1024], P(None, None, 'wa'), may hold values from -0.15625 to 0.15625
- up_weight: bfloat16 [8, 1536, 1024], P(None, None, 'wa'), may hold values from -0.15625 to 0.15625
- down_weight: bfloat16 [8, 1024, 1536], P(None, 'wa'), may hold values from -0.25 to 0.25
- cotangent: bfloat16 [4096, 1536], P('ctx'), may hold values from -6 to 6
Outputs:
- layer_output: float32 [4096, 1536], P('ctx')
- input_grad: float32 [4096, 1536], P('ctx')
- norm_gain_grad: float32 [1536], P('ctx')
- query_grad: float32 [1536, 1536], P('ctx', 'wa')
- key_grad: float32 [1536, 512], P('ctx', 'wa')
- value_grad: float32 [1536, 512], P('ctx', 'wa')
- output_grad: float32 [1536, 1536], P('wa', 'ctx')
- ffn_gain_grad: float32 [1536], P('ctx')
- router_grad: float32 [1536, 8], P('ctx')
- gate_grad: float32 [8, 1536, 1024], P(None, 'ctx', 'wa')
- up_grad: float32 [8, 1536, 1024], P(None, 'ctx', 'wa')
- down_grad: float32 [8, 1024, 1536], P(None, 'wa', 'ctx')
Inputs may be any that keep to these rules, and one draw needn't show every extreme that they name: `segment_ids`: segment ids never fall along the sequence; there are 5 documents, each of 64 tokens or more. `expert_ids`: among the 512 tokens of one index of ctx, no expert is named more than 256 times, a bound that some block reaches; a token's two experts differ.
All inputs are finite; a program needn't handle non-finite values.
Results may differ from a plain program's by a relative error of at most 0.03.
Values may be sent and summed in bfloat16 or wider, within the bound.
No kernel may reach another device: no remote copies, remote signals or barrier semaphores. Data moves between devices by JAX's collectives and lax.ppermute only.
A program may use at most 192 MiB of HBM per device.

v0:
```python
import math

import jax
import jax.numpy as jnp
from jax import lax
from jax.sharding import PartitionSpec as P

H = 24
KV = 8
HD = 64


eps = 1e-05
highest = lax.Precision.HIGHEST


def slot_table(routes, experts, capacity):
    flat = routes.reshape(-1)
    onehot = (flat[:, None] == jnp.arange(experts, dtype=jnp.int32)[None, :]).astype(jnp.int32)
    before = jnp.cumsum(onehot, axis=0) - onehot
    slots = jnp.sum(before * onehot, axis=1)
    position = flat * capacity + slots
    entries = jnp.arange(flat.shape[0], dtype=jnp.int32)
    owner = jnp.zeros((experts * capacity,), jnp.int32).at[position].set(entries)
    filled = jnp.zeros((experts * capacity,), jnp.int32).at[position].set(1)
    return (position, owner, filled)


def touching(seg_rows, seg_keys):
    return (seg_keys[0] <= seg_rows[-1]) & (seg_rows[0] <= seg_keys[-1])


def attend_block(running, queries, seg_rows, keys, values, seg_keys):

    def attend_compute(state_now):
        old_max, old_total, old_acc = state_now
        scores = jnp.einsum(
            "qngd,knd->ngqk", queries, keys, preferred_element_type=jnp.float32
        ) * HD ** (-0.5)
        same = (seg_rows[:, None] == seg_keys[None, :])[None, None]
        scores = jnp.where(same, scores, -1e30)
        new_max = jnp.maximum(old_max, jnp.max(scores, axis=-1))
        factor = jnp.exp(old_max - new_max)
        weights = jnp.where(same, jnp.exp(scores - new_max[..., None]), 0.0)
        new_total = old_total * factor + jnp.sum(weights, axis=-1)
        new_acc = old_acc * factor[..., None] + jnp.einsum(
            "ngqk,knd->ngqd",
            weights.astype(jnp.bfloat16),
            values,
            preferred_element_type=jnp.float32,
        )
        return (new_max, new_total, new_acc)

    def unchanged(state_now):
        return state_now

    return lax.cond(touching(seg_rows, seg_keys), attend_compute, unchanged, running)


def fold_keys(running, queries, seg_rows, key_rows, value_rows, seg_keys):
    total_rows = key_rows.shape[0]
    block_rows = math.gcd(total_rows, 1024)
    blocks = total_rows // block_rows

    def fold_visit(state_now, block_in):
        return (
            attend_block(state_now, queries, seg_rows, block_in[0], block_in[1], block_in[2]),
            None,
        )

    key_blocks = key_rows.reshape((blocks, block_rows) + key_rows.shape[1:])
    value_blocks = value_rows.reshape((blocks, block_rows) + value_rows.shape[1:])
    seg_blocks = seg_keys.reshape(blocks, block_rows)
    result, unused = lax.scan(fold_visit, running, (key_blocks, value_blocks, seg_blocks))
    return result


def guarded_grads(context, keys, values, seg_keys):
    queries, head_grad, log_total, offset, seg_rows = context

    def guarded_compute(operands):
        key_block, value_block = operands
        scores = jnp.einsum(
            "qngd,knd->ngqk", queries, key_block, preferred_element_type=jnp.float32
        ) * HD ** (-0.5)
        same = (seg_rows[:, None] == seg_keys[None, :])[None, None]
        probs = jnp.where(same, jnp.exp(scores - log_total[..., None]), 0.0)
        value_term = jnp.einsum(
            "ngqk,qngd->knd",
            probs.astype(jnp.bfloat16),
            head_grad,
            preferred_element_type=jnp.float32,
        )
        prob_grad = jnp.einsum(
            "qngd,knd->ngqk", head_grad, value_block, preferred_element_type=jnp.float32
        )
        score_grad = (probs * (prob_grad - offset[..., None])).astype(jnp.bfloat16)
        query_term = jnp.einsum(
            "ngqk,knd->qngd", score_grad, key_block, preferred_element_type=jnp.float32
        )
        key_term = jnp.einsum(
            "ngqk,qngd->knd", score_grad, queries, preferred_element_type=jnp.float32
        )
        return (query_term, key_term, value_term)

    def nothing(operands):
        return (
            jnp.zeros(queries.shape, jnp.float32),
            jnp.zeros(keys.shape, jnp.float32),
            jnp.zeros(values.shape, jnp.float32),
        )

    return lax.cond(touching(seg_rows, seg_keys), guarded_compute, nothing, (keys, values))


def grad_fold(context, key_rows, value_rows, seg_keys):
    total_rows = key_rows.shape[0]
    block_rows = math.gcd(total_rows, 1024)
    blocks = total_rows // block_rows

    def grad_visit(query_acc, block_in):
        query_term, key_term, value_term = guarded_grads(
            context, block_in[0], block_in[1], block_in[2]
        )
        return (query_acc + query_term, jnp.stack((key_term, value_term), 0))

    key_blocks = key_rows.reshape((blocks, block_rows) + key_rows.shape[1:])
    value_blocks = value_rows.reshape((blocks, block_rows) + value_rows.shape[1:])
    seg_blocks = seg_keys.reshape(blocks, block_rows)
    query_zero = jnp.zeros(context[0].shape, jnp.float32)
    query_acc, kv_blocks = lax.scan(grad_visit, query_zero, (key_blocks, value_blocks, seg_blocks))
    kv_terms = jnp.moveaxis(kv_blocks, 1, 0).reshape((2, total_rows) + key_rows.shape[1:])
    return (query_acc, kv_terms)


def per_device(
    layer_input,
    segment_ids,
    expert_ids,
    norm_gain,
    query_weight,
    key_weight,
    value_weight,
    output_weight,
    ffn_gain,
    router_weight,
    gate_weight,
    up_weight,
    down_weight,
    cotangent,
):
    tok_rows = layer_input.shape[0]
    model_width = layer_input.shape[1]
    groups = H // KV
    kv_local = key_weight.shape[1] // HD
    experts = gate_weight.shape[0]
    capacity = tok_rows // 2
    inputs = layer_input.astype(jnp.float32)
    seg_all = lax.all_gather(segment_ids, "ctx", axis=0, tiled=True)
    inv_one = lax.rsqrt(jnp.mean(inputs * inputs, axis=-1, keepdims=True) + eps)
    normed_one = (inputs * inv_one * norm_gain).astype(jnp.bfloat16)
    queries = (
        jnp.dot(normed_one, query_weight, preferred_element_type=jnp.float32)
        .astype(jnp.bfloat16)
        .reshape(tok_rows, kv_local, groups, HD)
    )
    keys = (
        jnp.dot(normed_one, key_weight, preferred_element_type=jnp.float32)
        .astype(jnp.bfloat16)
        .reshape(tok_rows, kv_local, HD)
    )
    values = (
        jnp.dot(normed_one, value_weight, preferred_element_type=jnp.float32)
        .astype(jnp.bfloat16)
        .reshape(tok_rows, kv_local, HD)
    )
    stacked = jnp.stack((keys, values), 0)
    start_state = (
        jnp.full((kv_local, groups, tok_rows), -1e30, jnp.float32),
        jnp.zeros((kv_local, groups, tok_rows), jnp.float32),
        jnp.zeros((kv_local, groups, tok_rows, HD), jnp.float32),
    )
    piece = lax.all_gather(stacked, "ctx", axis=1, tiled=True)
    seg_keys = seg_all
    running = fold_keys(start_state, queries, segment_ids, piece[0], piece[1], seg_keys)
    run_max, run_total, run_acc = running
    heads_f32 = jnp.transpose(run_acc / run_total[..., None], (2, 0, 1, 3))
    log_total = run_max + jnp.log(run_total)
    heads = heads_f32.astype(jnp.bfloat16).reshape(tok_rows, -1)
    attended = lax.psum(
        jnp.dot(heads, output_weight, preferred_element_type=jnp.float32).astype(jnp.bfloat16), "wa"
    ).astype(jnp.float32)
    hidden_one = inputs + attended
    inv_two = lax.rsqrt(jnp.mean(hidden_one * hidden_one, axis=-1, keepdims=True) + eps)
    normed_two = (hidden_one * inv_two * ffn_gain).astype(jnp.bfloat16)
    logits = jnp.dot(normed_two, router_weight, preferred_element_type=jnp.float32)
    picks = (expert_ids[:, :, None] == jnp.arange(experts, dtype=jnp.int32)[None, None, :]).astype(
        jnp.float32
    )
    chosen = jnp.sum(picks * logits[:, None, :], axis=-1)
    gates = jax.nn.softmax(chosen, axis=-1)
    position, owner, filled = slot_table(expert_ids, experts, capacity)
    slot_mask = filled.astype(jnp.bfloat16)[:, None]
    expert_in = (normed_two[owner // 2] * slot_mask).reshape(experts, capacity, model_width)
    gate_pre = jnp.einsum(
        "ecd,edf->ecf", expert_in, gate_weight, preferred_element_type=jnp.float32
    )
    up_pre = jnp.einsum("ecd,edf->ecf", expert_in, up_weight, preferred_element_type=jnp.float32)
    sigma = jax.nn.sigmoid(gate_pre)
    activated = gate_pre * sigma
    mids = (activated * up_pre).astype(jnp.bfloat16)
    expert_out = jnp.einsum(
        "ecf,efd->ecd", mids, down_weight, preferred_element_type=jnp.float32
    ).reshape(experts * capacity, model_width)
    per_token = expert_out[position].reshape(tok_rows, 2, model_width)
    mixed = lax.psum(
        jnp.sum(gates[:, :, None] * per_token, axis=1).astype(jnp.bfloat16), "wa"
    ).astype(jnp.float32)
    layer_output = hidden_one + mixed
    upstream = cotangent.astype(jnp.float32)
    gate_part = jnp.sum(upstream[:, None, :] * per_token, axis=-1)
    token_grads = (
        (gates[:, :, None] * upstream[:, None, :])
        .astype(jnp.bfloat16)
        .reshape(2 * tok_rows, model_width)
    )
    slot_grad = (token_grads[owner] * slot_mask).reshape(experts, capacity, model_width)
    mid_grad = jnp.einsum(
        "ecd,efd->ecf", slot_grad, down_weight, preferred_element_type=jnp.float32
    )
    up_back = (mid_grad * activated).astype(jnp.bfloat16)
    gate_pre_back = (mid_grad * up_pre * sigma * (1.0 + gate_pre * (1.0 - sigma))).astype(
        jnp.bfloat16
    )
    down_term = jnp.einsum("ecf,ecd->efd", mids, slot_grad, preferred_element_type=jnp.float32)
    gate_term = jnp.einsum(
        "ecd,ecf->edf", expert_in, gate_pre_back, preferred_element_type=jnp.float32
    )
    up_term = jnp.einsum("ecd,ecf->edf", expert_in, up_back, preferred_element_type=jnp.float32)
    input_slots = jnp.einsum(
        "ecf,edf->ecd", gate_pre_back, gate_weight, preferred_element_type=jnp.float32
    )
    input_slots = input_slots + jnp.einsum(
        "ecf,edf->ecd", up_back, up_weight, preferred_element_type=jnp.float32
    )
    normed_part = jnp.sum(
        input_slots.reshape(experts * capacity, model_width)[position].reshape(
            tok_rows, 2, model_width
        ),
        axis=1,
    )
    normed_back, gate_back = (
        lax.psum(normed_part.astype(jnp.bfloat16), "wa").astype(jnp.float32),
        lax.psum(gate_part.astype(jnp.bfloat16), "wa").astype(jnp.float32),
    )
    logit_pair = gates * (gate_back - jnp.sum(gates * gate_back, axis=-1, keepdims=True))
    logit_grad = jnp.sum(picks * logit_pair[:, :, None], axis=1)
    router_term = jnp.dot(normed_two.astype(jnp.float32).T, logit_grad, precision=highest)
    normed_back = normed_back + jnp.dot(
        logit_grad, router_weight.astype(jnp.float32).T, precision=highest
    )
    ffn_gain_term = jnp.sum(normed_back * hidden_one * inv_two, axis=0)
    scaled_two = normed_back * ffn_gain
    hidden_grad = upstream + inv_two * (
        scaled_two
        - hidden_one * inv_two * inv_two * jnp.mean(scaled_two * hidden_one, axis=-1, keepdims=True)
    )
    att_grad = hidden_grad.astype(jnp.bfloat16)
    head_grad = jnp.einsum(
        "td,qd->tq", att_grad, output_weight, preferred_element_type=jnp.float32
    ).astype(jnp.bfloat16)
    output_term = jnp.einsum("tq,td->qd", heads, att_grad, preferred_element_type=jnp.float32)
    head_grad = head_grad.reshape(tok_rows, kv_local, groups, HD)
    offset = jnp.transpose(jnp.sum(head_grad.astype(jnp.float32) * heads_f32, axis=-1), (1, 2, 0))
    context = (queries, head_grad, log_total, offset, segment_ids)
    piece = lax.all_gather(stacked, "ctx", axis=1, tiled=True)
    seg_keys = seg_all
    query_term, piece_terms = grad_fold(context, piece[0], piece[1], seg_keys)
    kv_grads = lax.psum_scatter(
        piece_terms.astype(jnp.bfloat16), "ctx", scatter_dimension=1, tiled=True
    ).astype(jnp.float32)
    score_scale = HD ** (-0.5)
    query_rows = (query_term * score_scale).astype(jnp.bfloat16).reshape(tok_rows, -1)
    key_rows = (kv_grads[0] * score_scale).astype(jnp.bfloat16).reshape(tok_rows, -1)
    value_rows = kv_grads[1].astype(jnp.bfloat16).reshape(tok_rows, -1)
    query_term_w = jnp.einsum(
        "td,tq->dq", normed_one, query_rows, preferred_element_type=jnp.float32
    )
    key_term_w = jnp.einsum("td,tq->dq", normed_one, key_rows, preferred_element_type=jnp.float32)
    value_term_w = jnp.einsum(
        "td,tq->dq", normed_one, value_rows, preferred_element_type=jnp.float32
    )
    normed_one_part = jnp.einsum(
        "tq,dq->td", query_rows, query_weight, preferred_element_type=jnp.float32
    )
    normed_one_part = normed_one_part + jnp.einsum(
        "tq,dq->td", key_rows, key_weight, preferred_element_type=jnp.float32
    )
    normed_one_part = normed_one_part + jnp.einsum(
        "tq,dq->td", value_rows, value_weight, preferred_element_type=jnp.float32
    )
    normed_one_back = lax.psum(normed_one_part.astype(jnp.bfloat16), "wa").astype(jnp.float32)
    norm_gain_term = jnp.sum(normed_one_back * inputs * inv_one, axis=0)
    scaled_one = normed_one_back * norm_gain
    input_grad = hidden_grad + inv_one * (
        scaled_one
        - inputs * inv_one * inv_one * jnp.mean(scaled_one * inputs, axis=-1, keepdims=True)
    )
    (
        query_sum,
        key_sum,
        value_sum,
        output_sum,
        norm_sum,
        gate_sum,
        up_sum,
        down_sum,
        router_sum,
        ffn_sum,
    ) = (
        lax.psum_scatter(
            query_term_w.astype(jnp.bfloat16), "ctx", scatter_dimension=0, tiled=True
        ).astype(jnp.float32),
        lax.psum_scatter(
            key_term_w.astype(jnp.bfloat16), "ctx", scatter_dimension=0, tiled=True
        ).astype(jnp.float32),
        lax.psum_scatter(
            value_term_w.astype(jnp.bfloat16), "ctx", scatter_dimension=0, tiled=True
        ).astype(jnp.float32),
        lax.psum_scatter(
            output_term.astype(jnp.bfloat16), "ctx", scatter_dimension=1, tiled=True
        ).astype(jnp.float32),
        lax.psum_scatter(
            norm_gain_term.astype(jnp.bfloat16), "ctx", scatter_dimension=0, tiled=True
        ).astype(jnp.float32),
        lax.psum_scatter(
            gate_term.astype(jnp.bfloat16), "ctx", scatter_dimension=1, tiled=True
        ).astype(jnp.float32),
        lax.psum_scatter(
            up_term.astype(jnp.bfloat16), "ctx", scatter_dimension=1, tiled=True
        ).astype(jnp.float32),
        lax.psum_scatter(
            down_term.astype(jnp.bfloat16), "ctx", scatter_dimension=2, tiled=True
        ).astype(jnp.float32),
        lax.psum_scatter(
            router_term.astype(jnp.bfloat16), "ctx", scatter_dimension=0, tiled=True
        ).astype(jnp.float32),
        lax.psum_scatter(
            ffn_gain_term.astype(jnp.bfloat16), "ctx", scatter_dimension=0, tiled=True
        ).astype(jnp.float32),
    )
    return (
        layer_output,
        input_grad,
        norm_sum,
        query_sum,
        key_sum,
        value_sum,
        output_sum,
        ffn_sum,
        router_sum,
        gate_sum,
        up_sum,
        down_sum,
    )


def solution(mesh):
    in_specs = (
        P("ctx", None),
        P("ctx"),
        P("ctx", None),
        P(),
        P(None, "wa"),
        P(None, "wa"),
        P(None, "wa"),
        P("wa", None),
        P(),
        P(),
        P(None, None, "wa"),
        P(None, None, "wa"),
        P(None, "wa", None),
        P("ctx", None),
    )
    out_specs = (
        P("ctx", None),
        P("ctx", None),
        P("ctx"),
        P("ctx", "wa"),
        P("ctx", "wa"),
        P("ctx", "wa"),
        P("wa", "ctx"),
        P("ctx"),
        P("ctx", None),
        P(None, "ctx", "wa"),
        P(None, "ctx", "wa"),
        P(None, "wa", "ctx"),
    )
    return jax.shard_map(
        per_device, mesh=mesh, in_specs=in_specs, out_specs=out_specs, check_vma=False
    )
```

profile of v0, /device:TPU:0, one launch (start us, length us, event | category | flops | bytes accessed | tf_op | source)
XLA Modules:
  0.0 1329.4 jit_solution(6180997431507281009)
XLA Ops:
  13.6 27.9 %all-gather = s32[8,1,512]{2,1,0:T(1,128)S(1)} all-gather(s32[1,1,512]{2,1,0:T(1,128)S(1)} %bitcast.221), channel_id=1, replica_groups=mesh['ctx'=8,'wa'=4] {'ctx'}, dimensions={0}, use_global_device_ids=true | all-gather | bytes 18432 | tf_op jit(solution)/shard_map/all_gather | solution.py:159
  47.0 20.9 %all-gather.3.cloned.1.call-done = bf16[2,4096,2,64]{1,3,2,0:T(8,128)(2,1)} async-done(((bf16[2,512,2,64]{1,3,2,0:T(8,128)(2,1)}), bf16[2,4096,2,64]{1,3,2,0:T(8,128)(2,1)}) %all-gather.3.cloned.1.call-update) | async-done | bytes 2097168 | tf_op jit(solution)/shard_map/all_gather | solution.py:183
  82.3 52.6 %while.27 = (s32[]{:T(128)}, f32[2,3,512]{2,1,0:T(4,128)S(1)}, f32[2,3,512]{2,1,0:T(4,128)S(1)}, f32[2,3,512,64]{2,3,1,0:T(8,128)}, s32[4,1024]{1,0:T(4,128)S(1)...) while((s32[]{:T(128)}, f32[2,3,512]{2,1,0:T(4,128)S(1)}, ...), condition=%wide.region_6.7_spmd, body=%wide.region_1.6_spmd.sunk | while | flops 847124480 | bytes 48840072 | solution.py:74
  118.5 12.5 conditional.5
  164.5 27.1 %all-reduce.8.cloned.1.call-done = bf16[512,1536]{1,0:T(8,128)(2,1)} async-done(((bf16[512,1536]{1,0:T(8,128)(2,1)}), bf16[512,1536]{1,0:T(8,128)(2,1)}) %all-reduce.8.cloned.1.call-update) | async-done | bytes 1572880 | tf_op jit(solution)/shard_map/psum | solution.py:190
  231.4 15.6 %gather_fusion.2 = bf16[2048,1536]{1,0:T(8,128)(2,1)} fusion(bf16[1024,1536]{1,0:T(8,128)(2,1)} %multiply_convert_fusion, s32[2048]{0:T(1024)S(1)} %get-tuple-element.476), kind=kCustom, calls=%fused_computation.2 | custom fusion | bytes 12591104 | tf_op jit(solution)/shard_map/gather | solution.py:227
  275.8 12.9 convolution_add_fusion
  330.1 12.7 gather_fusion.1
  351.0 16.2 %multiply_reduce_fusion = (bf16[512,2]{1,0:T(8,128)(2,1)}, bf16[512,1536]{1,0:T(8,128)(2,1)}) fusion(f32[512,2,1536]{2,1,0:T(2,128)} %reshape.290, f32[512,1536]{1,0:T(8,128)} %convert_element_type.210, f32[512,2]{1,0:T(8,128)S(1)} %copy.100), kind=kLoop, calls=%fused_computation.60 | loop fusion | flops 5504000 | bytes 11016192 | tf_op jit(solution)/shard_map/reduce_sum | solution.py:221
  383.2 90.2 %while.28 = (s32[]{:T(128)}, f32[512,2,3,64]{0,3,2,1:T(8,128)}, bf16[4,2,1024,2,64]{2,4,3,1,0:T(8,128)(2,1)}, s32[4,1024]{1,0:T(4,128)S(1)}, s32[512]{0:T(512)S(...) while((s32[]{:T(128)}, f32[512,2,3,64]{0,3,2,1:T(8,128)}, ...), condition=%wide.region_30.31_spmd.clone, body=%wide.region_27.30_spmd.clone.sunk | while | flops 2046689280 | bytes 65327432 | solution.py:131
  387.4 18.8 %conditional.6 = (f32[512,2,3,64]{0,3,2,1:T(8,128)}, bf16[1,1024,2,64]{1,3,2,0:T(8,128)(2,1)}, bf16[1,1024,2,64]{1,3,2,0:T(8,128)(2,1)S(1)}) conditional(s32[]{:T(128)} %convert_element_type.385, () %tuple.106, (s32[512]{0:T(512)S(1)}, s32[1,1024]{1,0:T(1,128)S(1)}, bf16[4,1024,2,64]{1,3,2,0:T(8,128)(2,1)}, s32[]{:T(128)}, ...), branch_computations={%region_28.28_spmd, %region_29.29_spmd} | conditional | flops 2045247488 | bytes 61910552 | solution.py:113
  413.9 18.8 %conditional.6 = (f32[512,2,3,64]{0,3,2,1:T(8,128)}, bf16[1,1024,2,64]{1,3,2,0:T(8,128)(2,1)}, bf16[1,1024,2,64]{1,3,2,0:T(8,128)(2,1)S(1)}) conditional(s32[]{:T(128)} %convert_element_type.385, () %tuple.106, (s32[512]{0:T(512)S(1)}, s32[1,1024]{1,0:T(1,128)S(1)}, bf16[4,1024,2,64]{1,3,2,0:T(8,128)(2,1)}, s32[]{:T(128)}, ...), branch_computations={%region_28.28_spmd, %region_29.29_spmd} | conditional | flops 2045247488 | bytes 61910552 | solution.py:113
  440.7 18.8 %conditional.6 = (f32[512,2,3,64]{0,3,2,1:T(8,128)}, bf16[1,1024,2,64]{1,3,2,0:T(8,128)(2,1)}, bf16[1,1024,2,64]{1,3,2,0:T(8,128)(2,1)S(1)}) conditional(s32[]{:T(128)} %convert_element_type.385, () %tuple.106, (s32[512]{0:T(512)S(1)}, s32[1,1024]{1,0:T(1,128)S(1)}, bf16[4,1024,2,64]{1,3,2,0:T(8,128)(2,1)}, s32[]{:T(128)}, ...), branch_computations={%region_28.28_spmd, %region_29.29_spmd} | conditional | flops 2045247488 | bytes 61910552 | solution.py:113
  486.1 75.5 %reduce-scatter.12.cloned.1.call-done = bf16[2,512,2,64]{1,3,2,0:T(8,128)(2,1)} async-done(((bf16[2,4096,2,64]{1,3,2,0:T(8,128)(2,1)}), bf16[2,512,2,64]{1,3,2,0:T(8,128)(2,1)}) %reduce-scatter.12.cloned.1.call-update) | async-done | bytes 262160 | tf_op jit(solution)/shard_map/reduce_scatter | solution.py:279
  596.6 28.6 %reduce-scatter.28.cloned.1.call-done = bf16[192,8]{1,0:T(8,128)(2,1)} async-done(((bf16[1536,8]{1,0:T(8,128)(2,1)}), bf16[192,8]{1,0:T(8,128)(2,1)}) %reduce-scatter.28.cloned.1.call-update) | async-done | bytes 3088
  626.7 64.9 %reduce-scatter.20.cloned.1.call-done = bf16[384,192]{0,1:T(8,128)(2,1)} async-done(((bf16[384,1536]{0,1:T(8,128)(2,1)}), bf16[384,192]{0,1:T(8,128)(2,1)}) %reduce-scatter.20.cloned.1.call-update) | async-done | bytes 147472 | tf_op jit(solution)/shard_map/reduce_scatter | solution.py:330
  693.2 65.3 %reduce-scatter.14.cloned.1.call-done = bf16[192,384]{1,0:T(8,128)(2,1)} async-done(((bf16[1536,384]{1,0:T(8,128)(2,1)}), bf16[192,384]{1,0:T(8,128)(2,1)}) %reduce-scatter.14.cloned.1.call-update) | async-done | bytes 147472 | tf_op jit(solution)/shard_map/reduce_scatter | solution.py:321
  760.2 62.1 %reduce-scatter.18.cloned.1.call-done = bf16[192,128]{1,0:T(8,128)(2,1)} async-done(((bf16[1536,128]{1,0:T(8,128)(2,1)}), bf16[192,128]{1,0:T(8,128)(2,1)}) %reduce-scatter.18.cloned.1.call-update) | async-done | bytes 49168 | tf_op jit(solution)/shard_map/reduce_scatter | solution.py:327
  823.7 62.8 %reduce-scatter.16.cloned.1.call-done = bf16[192,128]{1,0:T(8,128)(2,1)} async-done(((bf16[1536,128]{1,0:T(8,128)(2,1)}), bf16[192,128]{1,0:T(8,128)(2,1)}) %reduce-scatter.16.cloned.1.call-update) | async-done | bytes 49168 | tf_op jit(solution)/shard_map/reduce_scatter | solution.py:324
  887.9 69.0 %all-reduce.12.cloned.1.call-done = (bf16[512,1536]{1,0:T(8,128)(2,1)}, bf16[512,1536]{1,0:T(8,128)(2,1)}) async-done(((bf16[512,1536]{1,0:T(8,128)(2,1)}, bf16[512,1536]{1,0:T(8,128)(2,1)}), (bf16[512,1536]{1,0:T(8,128)(2,1)}, bf16[512,1536]{1,0:T(8,128)(2,1)})) %all-reduce.12.cloned.1.call-update) | async-done | bytes 3145744 | tf_op jit(solution)/shard_map/psum | solution.py:216
  959.6 22.1 %all-reduce.2 = (bf16[1536]{0:T(1024)(128)(2,1)S(1)}, bf16[1536]{0:T(1024)(128)(2,1)S(1)}) all-reduce(bf16[1536]{0:T(1024)(128)(2,1)S(1)} %get-tuple-element.411, bf16[1536]{0:T(1024)(128)(2,1)S(1)} %get-tuple-element.407), channel_id=3, replica_groups=mesh['ctx'=8,'wa'=4] {'ctx'}, use_global_device_ids=true, to_apply=%region_35.36.clone | all-reduce | flops 3072 | bytes 12288
  989.9 89.0 %reduce-scatter.26.cloned.1.call-done = bf16[8,256,192]{1,2,0:T(8,128)(2,1)} async-done(((bf16[8,256,1536]{1,2,0:T(8,128)(2,1)}), bf16[8,256,192]{1,2,0:T(8,128)(2,1)}) %reduce-scatter.26.cloned.1.call-update) | async-done | bytes 786448 | tf_op jit(solution)/shard_map/reduce_scatter | solution.py:342
  1081.4 118.2 %reduce-scatter.24.cloned.1.call-done = bf16[8,192,256]{2,1,0:T(8,128)(2,1)} async-done(((bf16[8,1536,256]{2,1,0:T(8,128)(2,1)}), bf16[8,192,256]{2,1,0:T(8,128)(2,1)}) %reduce-scatter.24.cloned.1.call-update) | async-done | bytes 786448 | tf_op jit(solution)/shard_map/reduce_scatter | solution.py:339
  1201.9 118.3 %reduce-scatter.22.cloned.1.call-done = bf16[8,192,256]{2,1,0:T(8,128)(2,1)} async-done(((bf16[8,1536,256]{2,1,0:T(8,128)(2,1)}), bf16[8,192,256]{2,1,0:T(8,128)(2,1)}) %reduce-scatter.22.cloned.1.call-update) | async-done | bytes 786448 | tf_op jit(solution)/shard_map/reduce_scatter | solution.py:336
  (300 shorter events, 409.7 us)
Async XLA Ops:
  7.2 129.6 %copy-start = (bf16[384,1536]{1,0:T(8,128)(2,1)S(1)}, bf16[384,1536]{1,0:T(8,128)(2,1)}, u32[]{:S(2)}) copy-start(bf16[384,1536]{1,0:T(8,128)(2,1)} %param.29) | copy-start | bytes 3538948
  7.2 60.7 %all-gather.3.cloned.1.call-start = ((), (), s32[]{:S(2)}) async-start(), calls=%async_computation.9 | async-start | bytes 2359296 | tf_op jit(solution)/shard_map/all_gather | solution.py:183
  9.2 35.5 %copy-start.32 = (f32[512]{0:T(512)}, f32[512]{0:T(512)S(1)}, u32[]{:S(2)}) copy-start(f32[512]{0:T(512)S(1)} %add_rsqrt_fusion.1) | copy-start | bytes 6148
  13.0 178.6 %all-reduce.8.cloned.1.call-start = ((), (), s32[]{:S(2)}) async-start(), calls=%async_computation.10 | async-start | bytes 3145728 | tf_op jit(solution)/shard_map/psum | solution.py:190
  139.0 235.1 %all-reduce.10.cloned.1.call-start = ((), (), s32[]{:S(2)}) async-start(), calls=%async_computation.11 | async-start | bytes 3145728 | tf_op jit(solution)/shard_map/psum | solution.py:253
  143.6 112.3 %copy-start.34 = (bf16[8,256]{1,0:T(8,128)(2,1)}, bf16[8,256]{1,0:T(8,128)(2,1)S(1)}, u32[]{:S(2)}) copy-start(bf16[8,256]{1,0:T(8,128)(2,1)S(1)} %mul.308) | copy-start | bytes 12292
  164.5 29.3 %copy-start.30 = (f32[1536]{0:T(1024)S(1)}, f32[1536]{0:T(1024)}, u32[]{:S(2)}) copy-start(f32[1536]{0:T(1024)} %param.30) | copy-start | bytes 18436
  194.6 11.2 copy-start.1
  214.4 8.2 copy-start.16
  214.4 14.9 %slice-start = ((s8[6291456]{0:T(1024)(128)(4,1)}), s8[4194304]{0:T(1024)(128)(4,1)S(1)}, s32[]{:S(2)}) async-start(s8[6291456]{0:T(1024)(128)(4,1)} %bitcast.209), calls=%async_computation.22 | async-start | bytes 8388608
  222.7 6.7 slice-start.1
  265.8 55.1 %copy-start.18 = (bf16[8,256,256]{2,1,0:T(8,128)(2,1)}, bf16[8,256,256]{2,1,0:T(8,128)(2,1)S(1)}, u32[]{:S(2)}) copy-start(bf16[8,256,256]{2,1,0:T(8,128)(2,1)S(1)} %get-tuple-element.471) | copy-start | bytes 3145732
  265.8 9.9 copy-start.22
  320.9 240.8 %reduce-scatter.12.cloned.1.call-start = ((), (), s32[]{:S(2)}) async-start(), calls=%async_computation.12 | async-start | bytes 2359296 | tf_op jit(solution)/shard_map/reduce_scatter | solution.py:279
  351.0 23.0 %copy-start.5 = (bf16[512,1536]{1,0:T(8,128)(2,1)S(1)}, bf16[512,1536]{1,0:T(8,128)(2,1)}, u32[]{:S(2)}) copy-start(bf16[512,1536]{1,0:T(8,128)(2,1)} %param.22) | copy-start | bytes 4718596
  476.7 148.5 %reduce-scatter.28.cloned.1.call-start = ((), (), s32[]{:S(2)}) async-start(), calls=%async_computation.20 | async-start | bytes 442368
  478.5 213.0 %reduce-scatter.20.cloned.1.call-start = ((), (), s32[]{:S(2)}) async-start(), calls=%async_computation.16 | async-start | bytes 1327104 | tf_op jit(solution)/shard_map/reduce_scatter | solution.py:330
  482.8 275.7 %reduce-scatter.14.cloned.1.call-start = ((), (), s32[]{:S(2)}) async-start(), calls=%async_computation.13 | async-start | bytes 1327104 | tf_op jit(solution)/shard_map/reduce_scatter | solution.py:321
  486.1 336.1 %reduce-scatter.18.cloned.1.call-start = ((), (), s32[]{:S(2)}) async-start(), calls=%async_computation.15 | async-start | bytes 442368 | tf_op jit(solution)/shard_map/reduce_scatter | solution.py:327
  564.2 322.3 %reduce-scatter.16.cloned.1.call-start = ((), (), s32[]{:S(2)}) async-start(), calls=%async_computation.14 | async-start | bytes 442368 | tf_op jit(solution)/shard_map/reduce_scatter | solution.py:324
  566.8 390.2 %all-reduce.12.cloned.1.call-start = ((), (), s32[]{:S(2)}) async-start(), calls=%async_computation.21 | async-start | bytes 6291456 | tf_op jit(solution)/shard_map/psum | solution.py:216
  572.0 507.0 %reduce-scatter.26.cloned.1.call-start = ((), (), s32[]{:S(2)}) async-start(), calls=%async_computation.19 | async-start | bytes 7077888 | tf_op jit(solution)/shard_map/reduce_scatter | solution.py:342
  579.6 619.9 %reduce-scatter.24.cloned.1.call-start = ((), (), s32[]{:S(2)}) async-start(), calls=%async_computation.18 | async-start | bytes 7077888 | tf_op jit(solution)/shard_map/reduce_scatter | solution.py:339
  587.2 733.1 %reduce-scatter.22.cloned.1.call-start = ((), (), s32[]{:S(2)}) async-start(), calls=%async_computation.17 | async-start | bytes 7077888 | tf_op jit(solution)/shard_map/reduce_scatter | solution.py:336
  (32 other events, 88.4 us)
Sparse Core Ops, SparseCore 0:
  13.1 54.6 all-gather.2
  139.1 52.4 all-reduce.7
  321.0 42.8 all-reduce.9
  476.9 84.7 reduce-scatter.11
  564.8 60.3 reduce-scatter.27
  628.4 63.0 reduce-scatter.19
  695.5 62.9 reduce-scatter.13
  761.8 60.3 reduce-scatter.17
  826.0 60.3 reduce-scatter.15
  889.3 67.6 all-reduce.11
  960.6 118.3 reduce-scatter.25
  1082.4 117.0 reduce-scatter.23
  1203.1 117.1 reduce-scatter.21
where the time goes:
time: 1340 us; the launch traced here: 1330 us
  waiting for transfers between devices  802 us (60%)
  matrix products  184 us (14%)
  local copies, waits for them, and re-layouts  149 us (11%)
  other arithmetic  101 us (8%)
  blocking collectives  55.8 us (4%)
  loops' own time  21.7 us (2%)
  between operations  15.4 us (1%)
    reduce_scatter x1, waiting for transfers between devices, per_device(): lax.psum_scatter(gate_term.astype(jnp.bfloat16), 'ctx', scatter_dimension...  118 us
    reduce_scatter x1, waiting for transfers between devices, per_device(): lax.psum_scatter(up_term.astype(jnp.bfloat16), 'ctx', scatter_dimension=1...  118 us
    reduce_scatter x1, waiting for transfers between devices, per_device(): lax.psum_scatter(down_term.astype(jnp.bfloat16), 'ctx', scatter_dimension...  89 us
    reduce_scatter x1, waiting for transfers between devices, per_device(): lax.psum_scatter(piece_terms.astype(jnp.bfloat16), 'ctx', scatter_dimensi...  75.5 us
    psum x1, waiting for transfers between devices, per_device(): lax.psum(jnp.sum(gates[:, :, None] * per_token, axis=1).astype(jnp.bfloat...  69 us
    reduce_scatter x1, waiting for transfers between devices, per_device(): lax.psum_scatter(query_term_w.astype(jnp.bfloat16), 'ctx', scatter_dimens...  65.3 us
    reduce_scatter x1, waiting for transfers between devices, per_device(): lax.psum_scatter(output_term.astype(jnp.bfloat16), 'ctx', scatter_dimensi...  64.9 us
    reduce_scatter x1, waiting for transfers between devices, per_device(): lax.psum_scatter(key_term_w.astype(jnp.bfloat16), 'ctx', scatter_dimensio...  62.8 us
  transfers between devices with their start and end apart: 13, of which 12 were waited for; matrix products, arithmetic and copies ran while one was open for 11% of the time, Pallas kernels for 0%

commit v1 on v0

v1 whole, which is shorter than its diff:
```python
import functools

import jax
import jax.numpy as jnp
from jax import lax
from jax.experimental import pallas as pl
from jax.experimental.pallas import tpu as pltpu
from jax.sharding import PartitionSpec as P

H = 24
KV = 8
HD = 64
eps = 1e-05
NEG = -1e30
F32 = jnp.float32
BF = jnp.bfloat16
VLIM = 60 * 1024 * 1024
EXTRA = 16
NT = (((1,), (1,)), ((), ()))
TN = (((0,), (0,)), ((), ()))


def digits_of(n):
    out = []
    stride = 1
    while n > 1:
        if stride == 1 and n % 2 == 0:
            radix = 2
        elif n % 4 == 0:
            radix = 4
        else:
            radix = n
        out.append((stride, radix))
        stride *= radix
        n //= radix
    return out


def moved(n, digit, shift):
    stride, radix = digit
    pairs = []
    for i in range(n):
        d = (i // stride) % radix
        pairs.append((i, i + ((d + shift) % radix - d) * stride))
    return pairs


def hop(x, n, digit, shift=1):
    return lax.ppermute(x, "ctx", moved(n, digit, shift))


def other_core(x):
    return lax.ppermute(x, "wa", [(i, i ^ 1) for i in range(4)])


def other_chip(x):
    return lax.ppermute(x, "wa", [(i, i ^ 2) for i in range(4)])


def rel_keys(digits):
    keys = [()]
    for _, radix in digits:
        keys = [k + (r,) for r in range(radix) for k in keys]
    return keys


def set_digit(key, at, value):
    return key[:at] + (value,) + key[at + 1 :]


def gather_ctx(x, n, digits, order):
    blocks = {tuple(0 for _ in digits): x}
    for at in order:
        fresh = {}
        for key, block in blocks.items():
            moving = block
            for s in range(1, digits[at][1]):
                moving = hop(moving, n, digits[at])
                fresh[set_digit(key, at, s)] = moving
        blocks.update(fresh)
    return blocks


def scatter_ctx(blocks, n, digits, order, add):
    for at in order:
        keys = list(blocks)
        rest = [k for k in keys if k[at] == 0]
        moving = {k: blocks[set_digit(k, at, 1 % digits[at][1])] for k in rest}
        for s in range(2, digits[at][1] + 1):
            stacked = jnp.stack([moving[k] for k in rest], 0) if len(rest) > 1 else moving[rest[0]]
            stacked = hop(stacked, n, digits[at])
            for i, k in enumerate(rest):
                got = stacked[i] if len(rest) > 1 else stacked
                moving[k] = add(got, blocks[set_digit(k, at, s % digits[at][1])])
        blocks = moving
    return blocks[tuple(0 for _ in digits)]


def add_bf(a, b):
    return (a.astype(F32) + b.astype(F32)).astype(BF)


def exchange_ctx(stack, n, digits):
    keys = rel_keys(digits)
    for at in range(len(digits)):
        parts = {i: stack[i] for i in range(len(keys))} if not isinstance(stack, dict) else stack
        for s in range(1, digits[at][1]):
            chosen = [i for i, k in enumerate(keys) if k[at] == s]
            bundle = jnp.stack([parts[i] for i in chosen], 0)
            bundle = hop(bundle, n, digits[at], s)
            for place, i in enumerate(chosen):
                parts[i] = bundle[place]
        stack = parts
    return stack


def digit_offset(me, key, digits, sign):
    place = 0
    for (stride, radix), r in zip(digits, key):
        d = (me // stride) % radix
        place = place + ((d + sign * r) % radix) * stride
    return place


def rel_rows(x, me, digits, rows, sign):
    return jnp.stack(
        [
            lax.dynamic_slice_in_dim(x, digit_offset(me, k, digits, sign) * rows, rows, 0)
            for k in rel_keys(digits)
        ],
        0,
    )


def params(**kw):
    return pltpu.CompilerParams(vmem_limit_bytes=VLIM, **kw)


def vspec(n):
    return [pl.BlockSpec(memory_space=pltpu.VMEM)] * n


def project_kernel(core_ref, x_ref, gain_ref, wq_ref, wk_ref, wv_ref, extra_ref, a1_ref, q_ref, kv_ref):
    tok = x_ref.shape[0]
    half = tok // 2
    kvw = wk_ref.shape[1]
    for i in range(2):
        start = pl.multiple_of(((core_ref[0] + i) % 2) * half, half)
        x = x_ref[pl.ds(start, half), :].astype(F32)
        inv = lax.rsqrt(jnp.mean(x * x, axis=-1, keepdims=True) + eps)
        a1 = (x * inv * gain_ref[...]).astype(BF)
        rows = pl.ds(i * half, half)
        a1_ref[rows, :] = a1
        kv_ref[rows, :kvw] = jnp.dot(a1, wk_ref[...], preferred_element_type=F32).astype(BF)
        kv_ref[rows, kvw:] = jnp.dot(a1, wv_ref[...], preferred_element_type=F32).astype(BF)
        q = jnp.dot(a1, wq_ref[...], preferred_element_type=F32).astype(BF)
        q_ref[rows, :] = (q.astype(F32) * HD ** (-0.5)).astype(BF)
    kv_ref[pl.ds(tok, EXTRA), :] = extra_ref[...]


def project(core, x, gain, wq, wk, wv, extra):
    tok, width = x.shape
    return pl.pallas_call(
        project_kernel,
        out_shape=(
            jax.ShapeDtypeStruct((tok, width), BF),
            jax.ShapeDtypeStruct((tok, wq.shape[1]), BF),
            jax.ShapeDtypeStruct((tok + EXTRA, 2 * wk.shape[1]), BF),
        ),
        in_specs=[pl.BlockSpec(memory_space=pltpu.SMEM)] + vspec(6),
        out_specs=tuple(vspec(3)),
        compiler_params=params(),
        name="project",
    )(core, x, gain, wq, wk, wv, extra)


def seg_onehot(row):
    lane = lax.broadcasted_iota(jnp.int32, (16, row.shape[1]), 0).astype(F32)
    return jnp.where(lane == row, 1.0, 0.0).astype(BF)


def seg_rows_of(block, tok):
    width = block.shape[1]
    return [
        block[tok : tok + EXTRA, :].astype(F32)[i : i + 1, :] for i in range(tok // width)
    ]


def attend_kernel(nb, heads, groups, *refs):
    q_ref = refs[0]
    kv_refs = refs[1 : 1 + nb]
    hf_ref, hb_ref, lse_ref = refs[1 + nb : 4 + nb]
    kv_s, q_s, m_s, l_s, acc_s = refs[4 + nb :]
    tok = q_ref.shape[0]
    kvw = kv_refs[0].shape[1] // 2
    for b in range(nb):
        kv_s[b] = kv_refs[b][...]
    for h in range(heads):
        q_s[h] = q_ref[:, h * HD : (h + 1) * HD]
    own = jnp.concatenate(seg_rows_of(kv_s[0], tok), axis=1)
    own_hot = seg_onehot(own)
    own_lo = jnp.min(own)
    own_hi = jnp.max(own)
    m_s[...] = jnp.full(m_s.shape, NEG, F32)
    l_s[...] = jnp.zeros(l_s.shape, F32)
    acc_s[...] = jnp.zeros(acc_s.shape, F32)

    def body(b, masked):
        block = kv_s[b]
        if masked:
            seg = jnp.concatenate(seg_rows_of(block, tok), axis=1)
            same = lax.dot_general(seg_onehot(seg), own_hot, TN, preferred_element_type=F32) > 0.5
        for n in range(heads // groups):
            k = block[:tok, n * HD : (n + 1) * HD]
            v = block[:tok, kvw + n * HD : kvw + (n + 1) * HD]
            for h in range(n * groups, (n + 1) * groups):
                s = lax.dot_general(k, q_s[h], NT, preferred_element_type=F32)
                if masked:
                    s = jnp.where(same, s, NEG)
                m_old = m_s[h : h + 1, :]
                m_new = jnp.maximum(m_old, jnp.max(s, axis=0, keepdims=True))
                p = jnp.exp(s - m_new)
                f = jnp.exp(m_old - m_new)
                m_s[h : h + 1, :] = m_new
                l_s[h : h + 1, :] = l_s[h : h + 1, :] * f + jnp.sum(p, axis=0, keepdims=True)
                acc_s[h] = acc_s[h] * f + lax.dot_general(
                    v, p.astype(BF), TN, preferred_element_type=F32
                )

    def visit(b, carry):
        seg = jnp.concatenate(seg_rows_of(kv_s[b], tok), axis=1)
        lo = jnp.min(seg)
        hi = jnp.max(seg)
        plain = (lo == hi) & (own_lo == own_hi) & (lo == own_lo)
        touch = (lo <= own_hi) & (own_lo <= hi)

        @pl.when(plain)
        def _():
            body(b, False)

        @pl.when(touch & jnp.logical_not(plain))
        def _():
            body(b, True)

        return carry

    lax.fori_loop(0, nb, visit, 0)
    rows = []
    for h in range(heads):
        rows.append(acc_s[h] / l_s[h : h + 1, :])
        lse_ref[h : h + 1, :] = m_s[h : h + 1, :] + jnp.log(l_s[h : h + 1, :])
    out = jnp.concatenate(rows, axis=0).T
    hf_ref[...] = out
    hb_ref[...] = out.astype(BF)


def attend(q, blocks, heads, groups):
    tok = q.shape[0]
    nb = len(blocks)
    return pl.pallas_call(
        functools.partial(attend_kernel, nb, heads, groups),
        out_shape=(
            jax.ShapeDtypeStruct((tok, heads * HD), F32),
            jax.ShapeDtypeStruct((tok, heads * HD), BF),
            jax.ShapeDtypeStruct((8, tok), F32),
        ),
        in_specs=vspec(1 + nb),
        out_specs=tuple(vspec(3)),
        scratch_shapes=[
            pltpu.VMEM((nb,) + blocks[0].shape, BF),
            pltpu.VMEM((heads, tok, HD), BF),
            pltpu.VMEM((8, tok), F32),
            pltpu.VMEM((8, tok), F32),
            pltpu.VMEM((heads, HD, tok), F32),
        ],
        compiler_params=params(),
        name="attend",
    )(q, *blocks)


def attend_back_kernel(nb, heads, groups, *refs):
    q_ref, do_ref, hf_ref, lse_ref = refs[:4]
    kv_refs = refs[4 : 4 + nb]
    dq_ref, dk_ref, dv_ref = refs[4 + nb : 7 + nb]
    kv_s, q_s, do_s, delta_s, dq_s = refs[7 + nb :]
    tok = q_ref.shape[0]
    kvw = kv_refs[0].shape[1] // 2
    for b in range(nb):
        kv_s[b] = kv_refs[b][...]
    for h in range(heads):
        q_s[h] = q_ref[:, h * HD : (h + 1) * HD]
        do_s[h] = do_ref[:, h * HD : (h + 1) * HD]
    prod = (do_ref[...].astype(F32) * hf_ref[...]).T
    for h in range(heads):
        delta_s[h : h + 1, :] = jnp.sum(prod[h * HD : (h + 1) * HD, :], axis=0, keepdims=True)
    own = jnp.concatenate(seg_rows_of(kv_s[0], tok), axis=1)
    own_hot = seg_onehot(own)
    own_lo = jnp.min(own)
    own_hi = jnp.max(own)
    dq_s[...] = jnp.zeros(dq_s.shape, F32)

    def body(b, masked):
        block = kv_s[b]
        if masked:
            seg = jnp.concatenate(seg_rows_of(block, tok), axis=1)
            same = lax.dot_general(seg_onehot(seg), own_hot, TN, preferred_element_type=F32) > 0.5
        for n in range(heads // groups):
            k = block[:tok, n * HD : (n + 1) * HD]
            v = block[:tok, kvw + n * HD : kvw + (n + 1) * HD]
            dk = None
            for h in range(n * groups, (n + 1) * groups):
                s = lax.dot_general(k, q_s[h], NT, preferred_element_type=F32)
                p = jnp.exp(s - lse_ref[h : h + 1, :])
                if masked:
                    p = jnp.where(same, p, 0.0)
                dv_h = jnp.dot(p.astype(BF), do_s[h], preferred_element_type=F32)
                dp = lax.dot_general(v, do_s[h], NT, preferred_element_type=F32)
                ds = (p * (dp - delta_s[h : h + 1, :])).astype(BF)
                dk_h = jnp.dot(ds, q_s[h], preferred_element_type=F32)
                dq_s[h] += lax.dot_general(k, ds, TN, preferred_element_type=F32)
                dk = dk_h if dk is None else dk + dk_h
                dv = dv_h if h == n * groups else dv + dv_h
            dk_ref[b, :, n * HD : (n + 1) * HD] = dk.astype(BF)
            dv_ref[b, :, n * HD : (n + 1) * HD] = dv.astype(BF)

    def visit(b, carry):
        seg = jnp.concatenate(seg_rows_of(kv_s[b], tok), axis=1)
        lo = jnp.min(seg)
        hi = jnp.max(seg)
        plain = (lo == hi) & (own_lo == own_hi) & (lo == own_lo)
        touch = (lo <= own_hi) & (own_lo <= hi)

        @pl.when(plain)
        def _():
            body(b, False)

        @pl.when(touch & jnp.logical_not(plain))
        def _():
            body(b, True)

        @pl.when(jnp.logical_not(touch))
        def _():
            dk_ref[b] = jnp.zeros(dk_ref.shape[1:], BF)
            dv_ref[b] = jnp.zeros(dv_ref.shape[1:], BF)

        return carry

    lax.fori_loop(0, nb, visit, 0)
    out = jnp.concatenate([dq_s[h] for h in range(heads)], axis=0).T
    dq_ref[...] = (out * HD ** (-0.5)).astype(BF)


def attend_back(q, do, hf, lse, blocks, heads, groups):
    tok = q.shape[0]
    nb = len(blocks)
    kvw = blocks[0].shape[1] // 2
    return pl.pallas_call(
        functools.partial(attend_back_kernel, nb, heads, groups),
        out_shape=(
            jax.ShapeDtypeStruct((tok, heads * HD), BF),
            jax.ShapeDtypeStruct((nb, tok, kvw), BF),
            jax.ShapeDtypeStruct((nb, tok, kvw), BF),
        ),
        in_specs=vspec(4 + nb),
        out_specs=tuple(vspec(3)),
        scratch_shapes=[
            pltpu.VMEM((nb,) + blocks[0].shape, BF),
            pltpu.VMEM((heads, tok, HD), BF),
            pltpu.VMEM((heads, tok, HD), BF),
            pltpu.VMEM((8, tok), F32),
            pltpu.VMEM((heads, HD, tok), F32),
        ],
        compiler_params=params(),
        name="attend_back",
    )(q, do, hf, lse, *blocks)


def experts_kernel(
    core_ref,
    ids_ref,
    mine_ref,
    theirs_ref,
    g_ref,
    wr_ref,
    wg_ref,
    wu_ref,
    wd_ref,
    mix_keep_ref,
    mix_send_ref,
    dx_keep_ref,
    dx_send_ref,
    gates_ref,
    ent_a_ref,
    ent_b_ref,
    a2_s,
    g_s,
    mix_s,
    dx_s,
    back_s,
):
    e = pl.program_id(0)
    tok, width = a2_s.shape
    half = tok // 2
    experts = wr_ref.shape[1]
    lane = lax.broadcasted_iota(jnp.int32, (tok, experts), 1)
    first = ids_ref[:, 0:1]
    second = ids_ref[:, 1:2]

    @pl.when(e == 0)
    def _():
        a2_s[:half, :] = mine_ref[...]
        a2_s[half:, :] = theirs_ref[...]
        for i in range(2):
            start = pl.multiple_of(((core_ref[0] + i) % 2) * half, half)
            g_s[pl.ds(i * half, half), :] = g_ref[pl.ds(start, half), :]
        logits = jnp.dot(a2_s[...], wr_ref[...], preferred_element_type=F32)
        one = jnp.sum(jnp.where(lane == first, logits, 0.0), axis=1, keepdims=True)
        two = jnp.sum(jnp.where(lane == second, logits, 0.0), axis=1, keepdims=True)
        top = jnp.maximum(one, two)
        one = jnp.exp(one - top)
        two = jnp.exp(two - top)
        total = one + two
        gates_ref[...] = jnp.where(lane == first, one / total, 0.0) + jnp.where(
            lane == second, two / total, 0.0
        )
        mix_s[...] = jnp.zeros(mix_s.shape, F32)
        dx_s[...] = jnp.zeros(dx_s.shape, F32)
        back_s[...] = jnp.zeros(back_s.shape, F32)
        ent_a_ref[...] = jnp.zeros(ent_a_ref.shape, BF)
        ent_b_ref[...] = jnp.zeros(ent_b_ref.shape, BF)

    wg = wg_ref[0]
    wu = wu_ref[0]
    wd = wd_ref[0]
    for i in range(2):
        rows = pl.ds(i * half, half)
        a2 = a2_s[rows, :]
        u = jnp.dot(a2, wg, preferred_element_type=F32)
        w = jnp.dot(a2, wu, preferred_element_type=F32)
        m = lax.dot_general(g_s[rows, :], wd, NT, preferred_element_type=F32)
        here = lane[:half] == e
        gate = jnp.sum(jnp.where(here, gates_ref[rows, :], 0.0), axis=1, keepdims=True)
        pick_one = (ids_ref[rows, 0:1] == e).astype(F32)
        pick_two = (ids_ref[rows, 1:2] == e).astype(F32)
        sig = 1.0 / (1.0 + jnp.exp(-u))
        act = u * sig
        mid = (act * w).astype(BF).astype(F32)
        back = jnp.sum(mid * m, axis=1, keepdims=True) * (pick_one + pick_two)
        back_s[rows, :] += jnp.where(here, back, 0.0)
        mid = mid * gate
        gm = gate * m
        up_back = gm * act
        pre_back = gm * w * sig * (1.0 + u * (1.0 - sig))
        mid_b = mid.astype(BF)
        up_b = up_back.astype(BF)
        pre_b = pre_back.astype(BF)
        mix_s[rows, :] += jnp.dot(mid_b, wd, preferred_element_type=F32)
        dx_s[rows, :] += lax.dot_general(
            pre_b, wg, NT, preferred_element_type=F32
        ) + lax.dot_general(up_b, wu, NT, preferred_element_type=F32)
        for kind, value in enumerate((mid, pre_back, up_back)):
            for c, pick in enumerate((pick_one, pick_two)):
                part = (value * pick).astype(BF)
                unit = 2 * kind + c
                if unit < 5:
                    ent_a_ref[unit, rows, :] += part
                else:
                    ent_b_ref[0, rows, :] += part

    @pl.when(e == pl.num_programs(0) - 1)
    def _():
        mix_keep_ref[...] = mix_s[:half, :]
        mix_send_ref[...] = mix_s[half:, :].astype(BF)
        dx_keep_ref[:, :width] = dx_s[:half, :]
        dx_send_ref[:, :width] = dx_s[half:, :].astype(BF)
        pad = jnp.zeros((half, 128 - experts), F32)
        dx_keep_ref[:, width:] = jnp.concatenate([back_s[:half, :], pad], axis=1)
        dx_send_ref[:, width:] = jnp.concatenate([back_s[half:, :], pad], axis=1).astype(BF)


def experts_call(core, ids, mine, theirs, g, wr, wg, wu, wd):
    half, width = mine.shape
    tok = 2 * half
    experts, _, hidden = wg.shape

    def whole(*shape):
        return pl.BlockSpec(shape, lambda e, *_: (0,) * len(shape))

    def one(*shape):
        return pl.BlockSpec((1,) + shape, lambda e, *_: (e,) + (0,) * len(shape))

    return pl.pallas_call(
        experts_kernel,
        out_shape=(
            jax.ShapeDtypeStruct((half, width), F32),
            jax.ShapeDtypeStruct((half, width), BF),
            jax.ShapeDtypeStruct((half, width + 128), F32),
            jax.ShapeDtypeStruct((half, width + 128), BF),
            jax.ShapeDtypeStruct((tok, experts), F32),
            jax.ShapeDtypeStruct((5, tok, hidden), BF),
            jax.ShapeDtypeStruct((1, tok, hidden), BF),
        ),
        grid=(experts,),
        in_specs=[
            pl.BlockSpec(memory_space=pltpu.SMEM),
            whole(tok, 2),
            whole(half, width),
            whole(half, width),
            whole(tok, width),
            whole(width, experts),
            one(width, hidden),
            one(width, hidden),
            one(hidden, width),
        ],
        out_specs=(
            whole(half, width),
            whole(half, width),
            whole(half, width + 128),
            whole(half, width + 128),
            whole(tok, experts),
            whole(5, tok, hidden),
            whole(1, tok, hidden),
        ),
        scratch_shapes=[
            pltpu.VMEM((tok, width), BF),
            pltpu.VMEM((tok, width), BF),
            pltpu.VMEM((tok, width), F32),
            pltpu.VMEM((tok, width), F32),
            pltpu.VMEM((tok, experts), F32),
        ],
        compiler_params=params(dimension_semantics=("arbitrary",)),
        name="experts",
    )(core, ids, mine, theirs, g, wr, wg, wu, wd)


def expert_grads_kernel(nb, seeded, *refs):
    ids_refs = refs[:nb]
    a_refs = refs[nb : 2 * nb]
    b_refs = refs[2 * nb : 3 * nb]
    xm_refs = refs[3 * nb : 4 * nb]
    xo_refs = refs[4 * nb : 5 * nb]
    gm_refs = refs[5 * nb : 6 * nb]
    go_refs = refs[6 * nb : 7 * nb]
    prev = refs[7 * nb : 7 * nb + 3] if seeded else None
    outs = refs[-3:]
    e = pl.program_id(0).astype(F32)
    sums = [None, None, None]
    for b in range(nb):
        half = xm_refs[b].shape[1]
        for i in range(2):
            rows = pl.ds(i * half, half)
            one = (ids_refs[b][rows, 0:1] == e).astype(F32)
            two = (ids_refs[b][rows, 1:2] == e).astype(F32)
            xt = (xm_refs if i == 0 else xo_refs)[b][...]
            gt = (gm_refs if i == 0 else go_refs)[b][...]
            for kind in range(3):
                left = a_refs[b][2 * kind, rows, :].astype(F32)
                right = (a_refs[b][2 * kind + 1, rows, :] if kind < 2 else b_refs[b][0, rows, :]).astype(F32)
                value = (left * one + right * two).astype(BF)
                term = jnp.dot(gt if kind == 0 else xt, value, preferred_element_type=F32)
                sums[kind] = term if sums[kind] is None else sums[kind] + term
    for kind in range(3):
        outs[kind][0] = sums[kind] + prev[kind][0] if seeded else sums[kind]


def expert_grads(ids, ent_a, ent_b, xm, xo, gm, go, experts, prev=None):
    nb = len(ids)
    cols = xm[0].shape[0]
    hidden = ent_a[0].shape[-1]
    operands = list(ids) + list(ent_a) + list(ent_b) + list(xm) + list(xo) + list(gm) + list(go)
    specs = [pl.BlockSpec(x.shape, lambda e, nd=x.ndim: (0,) * nd) for x in operands]
    out_spec = pl.BlockSpec((1, cols, hidden), lambda e: (e, 0, 0))
    if prev is not None:
        operands += list(prev)
        specs += [out_spec] * 3
    return pl.pallas_call(
        functools.partial(expert_grads_kernel, nb, prev is not None),
        out_shape=(jax.ShapeDtypeStruct((experts, cols, hidden), F32),) * 3,
        grid=(experts,),
        in_specs=specs,
        out_specs=(out_spec,) * 3,
        compiler_params=params(dimension_semantics=("arbitrary",)),
        name="expert_grads",
    )(*operands)


def per_device(
    n_ctx,
    layer_input,
    segment_ids,
    expert_ids,
    norm_gain,
    query_weight,
    key_weight,
    value_weight,
    output_weight,
    ffn_gain,
    router_weight,
    gate_weight,
    up_weight,
    down_weight,
    cotangent,
):
    tok, width = layer_input.shape
    half = tok // 2
    groups = H // KV
    kv_local = key_weight.shape[1] // HD
    heads = kv_local * groups
    kvw = key_weight.shape[1]
    experts = gate_weight.shape[0]
    cols = width // n_ctx
    digits = digits_of(n_ctx)
    keys = rel_keys(digits)
    upper_first = list(range(1, len(digits))) + [0]
    lower_first = list(range(len(digits)))
    me = lax.axis_index("ctx")
    core = lax.axis_index("wa") % 2
    core_arr = jnp.full((1,), core, jnp.int32)

    def mine_first(x):
        return jnp.where(core == 0, x, jnp.concatenate([x[half:], x[:half]], axis=0))

    def my_half(x):
        return lax.dynamic_slice_in_dim(x, core * half, half, 0)

    def whole_order(mine, theirs):
        return jnp.where(
            core == 0,
            jnp.concatenate([mine, theirs], axis=0),
            jnp.concatenate([theirs, mine], axis=0),
        )

    segs = mine_first(segment_ids).astype(BF)
    ids = mine_first(expert_ids)
    extra = jnp.concatenate([segs, ids[:, 0].astype(BF), ids[:, 1].astype(BF)])
    extra = jnp.pad(extra, (0, EXTRA * 2 * kvw - extra.shape[0])).reshape(EXTRA, 2 * kvw)
    a1, q, kv = project(
        core_arr, layer_input, norm_gain[None, :], query_weight, key_weight, value_weight, extra
    )
    kv_blocks = gather_ctx(kv, n_ctx, digits, upper_first)
    kv_list = [kv_blocks[k] for k in keys]
    heads_f32, heads_b, lse = attend(q, kv_list, heads, groups)

    used = tok // (2 * kvw)
    ids_list = []
    for block in kv_list:
        rows = block[tok + used : tok + 3 * used].astype(F32).reshape(2, tok)
        ids_list.append(rows.T)

    g_mine = my_half(cotangent)
    g_out = rel_rows(g_mine.T, me, digits, cols, 1)
    g_got = exchange_ctx(g_out, n_ctx, digits)
    g_stack = jnp.stack([g_got[i] for i in range(n_ctx)], 0)
    g_far = other_core(g_stack)

    far = jnp.dot(heads_b[half:], output_weight, preferred_element_type=F32).astype(BF)
    got = other_core(far)
    near = jnp.dot(heads_b[:half], output_weight, preferred_element_type=F32)
    near = (near + got.astype(F32)).astype(BF)
    got = other_chip(near)
    hidden_one = my_half(layer_input).astype(F32) + near.astype(F32) + got.astype(F32)
    inv_two = lax.rsqrt(jnp.mean(hidden_one * hidden_one, axis=-1, keepdims=True) + eps)
    a2_mine = (hidden_one * inv_two * ffn_gain).astype(BF)
    a2_far = other_core(a2_mine)
    a2_out = rel_rows(a2_mine.T, me, digits, cols, 1)
    a2_got = exchange_ctx(a2_out, n_ctx, digits)
    a2_stack = jnp.stack([a2_got[i] for i in range(n_ctx)], 0)
    a2_stack_far = other_core(a2_stack)

    mix_keep, mix_send, dx_keep, dx_send, gates, ent_a, ent_b = experts_call(
        core_arr,
        ids,
        a2_mine,
        a2_far,
        cotangent,
        router_weight,
        gate_weight,
        up_weight,
        down_weight,
    )
    ent_a_blocks = gather_ctx(ent_a, n_ctx, digits, upper_first)
    ent_b_blocks = gather_ctx(ent_b, n_ctx, digits, lower_first)

    near = (dx_keep + other_core(dx_send).astype(F32)).astype(BF)
    total = near.astype(F32) + other_chip(near).astype(F32)
    gate_back = total[:, width : width + experts]
    gate_half = gates[:half]
    picked = (
        (ids[:half, 0:1] == jnp.arange(experts)[None, :]) | (ids[:half, 1:2] == jnp.arange(experts)[None, :])
    ).astype(F32)
    logit_grad = picked * gate_half * (
        gate_back - jnp.sum(gate_half * gate_back, axis=-1, keepdims=True)
    )
    logit_b = logit_grad.astype(BF)
    normed_back = total[:, :width] + lax.dot_general(
        logit_b, router_weight, NT, preferred_element_type=F32
    )
    upstream = g_mine.astype(F32)
    ffn_term = jnp.sum(normed_back * hidden_one * inv_two, axis=0)
    scaled = normed_back * ffn_gain
    hidden_grad = upstream + inv_two * (
        scaled
        - hidden_one * inv_two * inv_two * jnp.mean(scaled * hidden_one, axis=-1, keepdims=True)
    )
    att_mine = hidden_grad.astype(BF)
    att_far = other_core(att_mine)
    att = jnp.concatenate([att_mine, att_far], axis=0)
    head_grad = lax.dot_general(att, output_weight, NT, preferred_element_type=F32).astype(BF)

    dq, dk, dv = attend_back(q, head_grad, heads_f32, lse, kv_list, heads, groups)
    dk_sum = scatter_ctx(
        {k: dk[i] for i, k in enumerate(keys)}, n_ctx, digits, lower_first, add_bf
    )
    dv_sum = scatter_ctx(
        {k: dv[i] for i, k in enumerate(keys)}, n_ctx, digits, upper_first, add_bf
    )

    part = (
        lax.dot_general(dq, query_weight, NT, preferred_element_type=F32)
        + lax.dot_general(dk_sum, key_weight, NT, preferred_element_type=F32)
        + lax.dot_general(dv_sum, value_weight, NT, preferred_element_type=F32)
    )
    near = (part[:half] + other_core(part[half:].astype(BF)).astype(F32)).astype(BF)
    normed_back = near.astype(F32) + other_chip(near).astype(F32)
    x_mine = my_half(layer_input).astype(F32)
    inv_one = lax.rsqrt(jnp.mean(x_mine * x_mine, axis=-1, keepdims=True) + eps)
    norm_term = jnp.sum(normed_back * x_mine * inv_one, axis=0)
    scaled = normed_back * norm_gain
    in_mine = hidden_grad + inv_one * (
        scaled - x_mine * inv_one * inv_one * jnp.mean(scaled * x_mine, axis=-1, keepdims=True)
    )
    input_grad = whole_order(in_mine, other_core(in_mine))

    near = (mix_keep + other_core(mix_send).astype(F32)).astype(BF)
    out_mine = hidden_one + near.astype(F32) + other_chip(near).astype(F32)
    layer_output = whole_order(out_mine, other_core(out_mine))

    a1_rel = rel_rows(a1.T, me, digits, cols, -1).reshape(width, tok)
    att_rel = rel_rows(att.T, me, digits, cols, -1).reshape(width, tok)
    a2_rel = rel_rows(a2_mine.T, me, digits, cols, -1).reshape(width, half)
    ffn_rel = rel_rows(ffn_term[:, None], me, digits, cols, -1).reshape(width, 1)
    norm_rel = rel_rows(norm_term[:, None], me, digits, cols, -1).reshape(width, 1)
    out_term = jnp.dot(att_rel, heads_b, preferred_element_type=F32)
    router_term = jnp.dot(a2_rel, logit_b, preferred_element_type=F32)
    pad = jnp.zeros((width, 128 - experts - 1), F32)
    early = jnp.concatenate([out_term, router_term, ffn_rel, pad], axis=1).astype(BF)
    early = early.reshape(n_ctx, cols, early.shape[1])
    rows = jnp.concatenate([dq, dk_sum, dv_sum], axis=1)
    late = jnp.dot(a1_rel, rows, preferred_element_type=F32)
    pad = jnp.zeros((width, 127), F32)
    late = jnp.concatenate([late, norm_rel, pad], axis=1).astype(BF)
    late = late.reshape(n_ctx, cols, late.shape[1])
    early = scatter_ctx(
        {k: early[i] for i, k in enumerate(keys)}, n_ctx, digits, lower_first, add_bf
    ).astype(F32)
    late = scatter_ctx(
        {k: late[i] for i, k in enumerate(keys)}, n_ctx, digits, lower_first, add_bf
    ).astype(F32)
    qw = heads * HD
    output_grad = early[:, :qw].T
    small = jnp.concatenate(
        [early[:, qw : qw + experts + 1], late[:, qw + 2 * kvw : qw + 2 * kvw + 1]], axis=1
    )
    small = small + other_core(small)
    router_grad = small[:, :experts]
    ffn_grad = small[:, experts]
    norm_grad = small[:, experts + 1]
    query_grad = late[:, :qw]
    key_grad = late[:, qw : qw + kvw]
    value_grad = late[:, qw + kvw : qw + 2 * kvw]

    sums = None
    for at in range(0, n_ctx, 8):
        some = range(at, min(at + 8, n_ctx))
        sums = expert_grads(
            [ids_list[i] for i in some],
            [ent_a_blocks[keys[i]] for i in some],
            [ent_b_blocks[keys[i]] for i in some],
            [a2_stack[i] for i in some],
            [a2_stack_far[i] for i in some],
            [g_stack[i] for i in some],
            [g_far[i] for i in some],
            experts,
            sums,
        )
    down_grad, gate_grad, up_grad = sums
    down_grad = jnp.swapaxes(down_grad, 1, 2)
    return (
        layer_output,
        input_grad,
        norm_grad,
        query_grad,
        key_grad,
        value_grad,
        output_grad,
        ffn_grad,
        router_grad,
        gate_grad,
        up_grad,
        down_grad,
    )


def solution(mesh):
    in_specs = (
        P("ctx", None),
        P("ctx"),
        P("ctx", None),
        P(),
        P(None, "wa"),
        P(None, "wa"),
        P(None, "wa"),
        P("wa", None),
        P(),
        P(),
        P(None, None, "wa"),
        P(None, None, "wa"),
        P(None, "wa", None),
        P("ctx", None),
    )
    out_specs = (
        P("ctx", None),
        P("ctx", None),
        P("ctx"),
        P("ctx", "wa"),
        P("ctx", "wa"),
        P("ctx", "wa"),
        P("wa", "ctx"),
        P("ctx"),
        P("ctx", None),
        P(None, "ctx", "wa"),
        P(None, "ctx", "wa"),
        P(None, "wa", "ctx"),
    )
    return jax.shard_map(
        functools.partial(per_device, mesh.shape["ctx"]),
        mesh=mesh,
        in_specs=in_specs,
        out_specs=out_specs,
        check_vma=False,
    )
```

time: 1340 us -> 648 us (0.48)
  waiting for transfers between devices: 802 us -> 241 us
  matrix products: 184 us -> 13.1 us
  Pallas kernels: 0 us -> 131 us
  starting transfers between devices: 0.93 us -> 72.8 us
  blocking collectives: 55.8 us -> 0 us
  other arithmetic: 101 us -> 59.1 us
  local copies, waits for them, and re-layouts: 149 us -> 120 us
  loops' own time: 21.7 us -> 0 us
    reduce_scatter x8 -> x0, waiting for transfers between devices: 656 us -> none  [the longest x1 118 us: per_device(): lax.psum_scatter(gate_term.astype(jnp.bfloat16), 'ctx', scatter_dimension...]
    ppermute x0 -> x60, waiting for transfers between devices: none -> 241 us  [the longest x45 196 us: hop(): return lax.ppermute(x, 'ctx', moved(n, digit, shift))]
    dot_general x45 -> x10, matrix products: 184 us -> 13.1 us  [the longest x1 3.55 us: per_device(): late = jnp.dot(a1_rel, rows, preferred_element_type=F32)]
    pallas_call x0 -> x5, Pallas kernels: none -> 131 us  [the longest x1 35.2 us: attend_back(): pl.pallas_call(functools.partial(attend_back_kernel, nb, heads, groups),...]
    psum x3 -> x0, waiting for transfers between devices: 96.2 us -> none  [the longest x1 69 us: per_device(): lax.psum(jnp.sum(gates[:, :, None] * per_token, axis=1).astype(jnp.bfloat...]
    ppermute x0 -> x60, starting transfers between devices: none -> 72.8 us  [the longest x45 66.3 us: hop(): return lax.ppermute(x, 'ctx', moved(n, digit, shift))]
    gather x6 -> x0, local copies, waits for them, and re-layouts: 68.5 us -> none  [the longest x2 24.6 us: per_device(): token_grads[owner] * slot_mask]
    unnamed x78 -> x160, local copies, waits for them, and re-layouts: 7.58 us -> 52.9 us
  transfers between devices with their start and end apart: 13 -> 60, of which waited for: 12 -> 24; matrix products, arithmetic and copies ran while one was open for 11% -> 28% of each run, Pallas kernels for 0% -> 20%
where the time goes in v1:
time: 648 us; the launch traced here: 640 us
  waiting for transfers between devices  241 us (37%)
  Pallas kernels  131 us (20%)
  local copies, waits for them, and re-layouts  120 us (19%)
  starting transfers between devices  72.8 us (11%)
  other arithmetic  59.1 us (9%)
  matrix products  13.1 us (2%)
    ppermute x45, waiting for transfers between devices, hop(): return lax.ppermute(x, 'ctx', moved(n, digit, shift))  196 us
    ppermute x45, starting transfers between devices, hop(): return lax.ppermute(x, 'ctx', moved(n, digit, shift))  66.3 us
    unnamed x160, local copies, waits for them, and re-layouts  52.9 us
    ppermute x4, waiting for transfers between devices, other_chip(): return lax.ppermute(x, 'wa', [(i, i ^ 2) for i in range(4)])  45.3 us
    pallas_call x1, Pallas kernels, attend_back(): pl.pallas_call(functools.partial(attend_back_kernel, nb, heads, groups),...  35.2 us
    pallas_call x1, Pallas kernels, experts_call(): pl.pallas_call(experts_kernel, out_shape=(jax.ShapeDtypeStruct((half, wid...  32.6 us
    pallas_call x1, Pallas kernels, expert_grads(): pl.pallas_call(functools.partial(expert_grads_kernel, nb, prev is not Non...  30.5 us
    pallas_call x1, Pallas kernels, attend(): pl.pallas_call(functools.partial(attend_kernel, nb, heads, groups), out_s...  27.7 us
  transfers between devices with their start and end apart: 60, of which 24 were waited for; matrix products, arithmetic and copies ran while one was open for 28% of the time, Pallas kernels for 20%

profile of v1, /device:TPU:0, one launch (start us, length us, event | category | flops | bytes accessed | tf_op | source)
XLA Modules:
  0.0 639.6 jit_solution(9587977784930811326)
XLA Ops:
  5.4 5.0 project.1
  69.3 8.9 %collective-permute-done.5.refs_7_.refs_10_ = bf16[528,256]{1,0:T(8,128)(2,1)S(1)} collective-permute-done((bf16[528,256]{1,0:T(8,128)(2,1)S(1)}, bf16[528,256]{1,0:T(8,128)(2,1)S(1)}, u32[]{:S(2)}, u32[]{:S(2)}) %collective-permute-start.5) | collective-permute-done | bytes 270368 | tf_op jit(solution)/shard_map/ppermute | solution.py:49
  84.8 27.7 %attend.1 = (f32[512,384]{1,0:T(8,128)}, bf16[512,384]{1,0:T(8,128)(2,1)}, f32[8,512]{1,0:T(8,128)}) custom-call(bf16[512,384]{1,0:T(8,128)(2,1)} %get-tuple-element.31.refs_0_, bf16[528,256]{1,0:T(8,128)(2,1)} %get-tuple-element.32.refs_1_.refs_4_, bf16[528,256]{1,0:T(8,128)(2,1)} %collective-permute-done.refs_2_.refs_5_, ...), custom_call_target="tpu_custom_call" | custom-call | tf_op jit(solution)/shard_map/attend/pallas_call | solution.py:260
  128.2 12.4 %collective-permute-done.8 = bf16[256,1536]{0,1:T(8,128)(2,1)} collective-permute-done((bf16[256,1536]{0,1:T(8,128)(2,1)S(1)}, bf16[256,1536]{0,1:T(8,128)(2,1)}, u32[]{:S(2)}, u32[]{:S(2)}) %collective-permute-start.8) | collective-permute-done | bytes 786464 | tf_op jit(solution)/shard_map/ppermute | solution.py:57
  154.3 32.6 %experts.1 = (f32[256,1536]{1,0:T(8,128)}, bf16[256,1536]{1,0:T(8,128)(2,1)}, f32[256,1664]{1,0:T(8,128)}, bf16[256,1664]{1,0:T(8,128)(2,1)}, f32[512,8]{1,0:T(8...) custom-call(s32[1]{0:T(128)} %bitcast.core_ref, s32[512,2]{1,0:T(8,128)} %get-tuple-element.99.ids_ref, ...), custom_call_target="tpu_custom_call" | custom-call | tf_op jit(solution)/shard_map/experts/pallas_call | solution.py:492
  198.6 11.9 %collective-permute-start.52 = (bf16[2,192,256]{2,1,0:T(8,128)(2,1)}, bf16[2,192,256]{2,1,0:T(8,128)(2,1)}, u32[]{:S(2)}, u32[]{:S(2)}) collective-permute-start(bf16[2,192,256]{2,1,0:T(8,128)(2,1)} %pad_maximum_fusion.12), channel_id=1, source_target_pairs={{0,16},{4,20},{8,24},{12,28},{16,0},{20,4},{24,8},{28,12},{1,17},{... | collective-permute-start | bytes 589832 | tf_op jit(solution)/shard_map/ppermute | solution.py:49
  232.0 7.3 %collective-permute-done.14 = bf16[256,1664]{0,1:T(8,128)(2,1)} collective-permute-done((bf16[256,1664]{0,1:T(8,128)(2,1)}, bf16[256,1664]{0,1:T(8,128)(2,1)}, u32[]{:S(2)}, u32[]{:S(2)}) %collective-permute-start.14) | collective-permute-done | bytes 852000 | tf_op jit(solution)/shard_map/ppermute | solution.py:57
  242.0 13.6 %collective-permute-done.11 = bf16[256,1536]{0,1:T(8,128)(2,1)S(1)} collective-permute-done((bf16[256,1536]{0,1:T(8,128)(2,1)S(1)}, bf16[256,1536]{0,1:T(8,128)(2,1)S(1)}, u32[]{:S(2)}, u32[]{:S(2)}) %collective-permute-start.11) | collective-permute-done | bytes 786464 | tf_op jit(solution)/shard_map/ppermute | solution.py:57
  266.3 35.2 %attend_back.1 = (bf16[512,384]{1,0:T(8,128)(2,1)}, bf16[8,512,128]{2,1,0:T(8,128)(2,1)}, bf16[8,512,128]{2,1,0:T(8,128)(2,1)}) custom-call(bf16[512,384]{1,0:T(8,128)(2,1)} %get-tuple-element.31.refs_0_, bf16[512,384]{1,0:T(8,128)(2,1)} %fusion.15.refs_1_, f32[512,384]{1,0:T(8,128)} %get-tuple-element.39.refs_2_, f32[8,512]{1,0:T(8,128)} %get-tuple-element.40.refs_3_, ...), custom_call_target="tpu_custom_call" | custom-call | tf_op jit(solution)/shard_map/attend_back/pallas_call | solution.py:357
  304.9 7.6 %collective-permute-done.20 = bf16[2,512,128]{2,1,0:T(8,128)(2,1)S(1)} collective-permute-done((bf16[2,512,128]{2,1,0:T(8,128)(2,1)S(1)}, bf16[2,512,128]{2,1,0:T(8,128)(2,1)S(1)}, u32[]{:S(2)}, u32[]{:S(2)}) %collective-permute-start.20) | collective-permute-done | bytes 262176 | tf_op jit(solution)/shard_map/ppermute | solution.py:49
  312.7 7.6 %collective-permute-start.21 = (bf16[2,512,128]{2,1,0:T(8,128)(2,1)S(1)}, bf16[2,512,128]{2,1,0:T(8,128)(2,1)S(1)}, u32[]{:S(2)}, u32[]{:S(2)}) collective-permute-start(bf16[2,512,128]{2,1,0:T(8,128)(2,1)S(1)} %pad_maximum_fusion.9), channel_id=1, source_target_pairs={{0,8},{4,12},{8,16},{12,20},{16,24},{20,28},{24,0},{28,4},{1,9},{5... | collective-permute-start | bytes 786440 | tf_op jit(solution)/shard_map/ppermute | solution.py:49
  331.9 6.7 %collective-permute-done.17 = bf16[512,128]{1,0:T(8,128)(2,1)S(1)} collective-permute-done((bf16[512,128]{1,0:T(8,128)(2,1)S(1)}, bf16[512,128]{1,0:T(8,128)(2,1)S(1)}, u32[]{:S(2)}, u32[]{:S(2)}) %collective-permute-start.17) | collective-permute-done | bytes 131104 | tf_op jit(solution)/shard_map/ppermute | solution.py:49
  340.6 32.8 %collective-permute-done.18 = bf16[512,128]{1,0:T(8,128)(2,1)S(1)} collective-permute-done((bf16[512,128]{1,0:T(8,128)(2,1)S(1)}, bf16[512,128]{1,0:T(8,128)(2,1)S(1)}, u32[]{:S(2)}, u32[]{:S(2)}) %collective-permute-start.18) | collective-permute-done | bytes 131104 | tf_op jit(solution)/shard_map/ppermute | solution.py:49
  373.4 5.8 collective-permute-start.23
  383.1 6.0 collective-permute-done.19
  407.8 11.9 %collective-permute-done.27 = bf16[4,192,512]{2,1,0:T(8,128)(2,1)S(1)} collective-permute-done((bf16[4,192,512]{2,1,0:T(8,128)(2,1)}, bf16[4,192,512]{2,1,0:T(8,128)(2,1)S(1)}, u32[]{:S(2)}, u32[]{:S(2)}) %collective-permute-start.27) | collective-permute-done | bytes 786464 | tf_op jit(solution)/shard_map/ppermute | solution.py:49
  427.4 12.0 %collective-permute-done.25 = bf16[256,1536]{0,1:T(8,128)(2,1)S(1)} collective-permute-done((bf16[256,1536]{0,1:T(8,128)(2,1)}, bf16[256,1536]{0,1:T(8,128)(2,1)S(1)}, u32[]{:S(2)}, u32[]{:S(2)}) %collective-permute-start.25) | collective-permute-done | bytes 786464 | tf_op jit(solution)/shard_map/ppermute | solution.py:57
  460.3 18.2 %collective-permute-done.31 = bf16[4,192,768]{2,1,0:T(8,128)(2,1)} collective-permute-done((bf16[4,192,768]{2,1,0:T(8,128)(2,1)}, bf16[4,192,768]{2,1,0:T(8,128)(2,1)}, u32[]{:S(2)}, u32[]{:S(2)}) %collective-permute-start.31) | collective-permute-done | bytes 1179680 | tf_op jit(solution)/shard_map/ppermute | solution.py:49
  481.7 14.2 %collective-permute-done.48.refs_22_ = bf16[1,512,256]{2,1,0:T(8,128)(2,1)} collective-permute-done((bf16[1,512,256]{2,1,0:T(8,128)(2,1)}, bf16[1,512,256]{2,1,0:T(8,128)(2,1)}, u32[]{:S(2)}, u32[]{:S(2)}) %collective-permute-start.48) | collective-permute-done | bytes 262176 | tf_op jit(solution)/shard_map/ppermute | solution.py:49
  508.1 5.3 maximum_select_fusion
  524.6 8.8 %collective-permute-done.30 = bf16[192,512]{0,1:T(8,128)(2,1)S(1)} collective-permute-done((bf16[192,512]{0,1:T(8,128)(2,1)}, bf16[192,512]{0,1:T(8,128)(2,1)S(1)}, u32[]{:S(2)}, u32[]{:S(2)}) %collective-permute-start.30) | collective-permute-done | bytes 196640 | tf_op jit(solution)/shard_map/ppermute | solution.py:49
  535.5 26.4 %collective-permute-done.40.refs_13_ = bf16[5,512,256]{2,1,0:T(8,128)(2,1)} collective-permute-done((bf16[5,512,256]{2,1,0:T(8,128)(2,1)}, bf16[5,512,256]{2,1,0:T(8,128)(2,1)}, u32[]{:S(2)}, u32[]{:S(2)}) %collective-permute-start.40) | collective-permute-done | bytes 1310752 | tf_op jit(solution)/shard_map/ppermute | solution.py:49
  561.9 27.2 %collective-permute-done.42.refs_15_ = bf16[5,512,256]{2,1,0:T(8,128)(2,1)} collective-permute-done((bf16[5,512,256]{2,1,0:T(8,128)(2,1)}, bf16[5,512,256]{2,1,0:T(8,128)(2,1)}, u32[]{:S(2)}, u32[]{:S(2)}) %collective-permute-start.42) | collective-permute-done | bytes 1310752 | tf_op jit(solution)/shard_map/ppermute | solution.py:49
  589.1 30.5 %expert_grads.1 = (f32[8,192,256]{2,1,0:T(8,128)}, f32[8,192,256]{2,1,0:T(8,128)}, f32[8,192,256]{2,1,0:T(8,128)}) custom-call(f32[512,2]{1,0:T(8,128)} %bitcast.311, f32[512,2]{1,0:T(8,128)} %bitcast.312, f32[512,2]{1,0:T(8,128)} %bitcast.313, f32[512,2]{1,0:T(8,128)} %bitcast.314, f32[512,2]{1,0:T(8,128)} %bitcast.315, f32[512,2]{1,0:T(8,128)} %bitcast.316, ...), custom_call_target="tpu_custom_call" | custom-call | tf_op jit(solution)/shard_map/expert_grads/pallas_call | solution.py:576
  (429 shorter events, 261.7 us)
Async XLA Ops:
  10.4 37.6 %collective-permute-start = (bf16[528,256]{1,0:T(8,128)(2,1)}, bf16[528,256]{1,0:T(8,128)(2,1)}, u32[]{:S(2)}, u32[]{:S(2)}) collective-permute-start(bf16[528,256]{1,0:T(8,128)(2,1)} %get-tuple-element.32.refs_1_.refs_4_), channel_id=1, source_target_pairs={{0,4},{4,0},{8,12},{12,8},{16,20},{20,16},{24,28},{28,24},{1,5},{5... | collective-permute-start | bytes 811016 | tf_op jit(solution)/shard_map/ppermute | solution.py:49
  13.4 36.3 %collective-permute-start.1 = (bf16[528,256]{1,0:T(8,128)(2,1)}, bf16[528,256]{1,0:T(8,128)(2,1)}, u32[]{:S(2)}, u32[]{:S(2)}) collective-permute-start(bf16[528,256]{1,0:T(8,128)(2,1)} %get-tuple-element.32.refs_1_.refs_4_), channel_id=1, source_target_pairs={{0,8},{4,12},{8,16},{12,20},{16,24},{20,28},{24,0},{28,4},{1,9},{5... | collective-permute-start | bytes 811016 | tf_op jit(solution)/shard_map/ppermute | solution.py:49
  17.8 36.6 %collective-permute-start.55 = (bf16[4,192,256]{2,1,0:T(8,128)(2,1)}, bf16[4,192,256]{2,1,0:T(8,128)(2,1)}, u32[]{:S(2)}, u32[]{:S(2)}) collective-permute-start(bf16[4,192,256]{2,1,0:T(8,128)(2,1)} %pad_maximum_fusion.8), channel_id=1, source_target_pairs={{0,4},{4,0},{8,12},{12,8},{16,20},{20,16},{24,28},{28,24},{1,5},{5... | collective-permute-start | bytes 1179656 | tf_op jit(solution)/shard_map/ppermute | solution.py:49
  64.8 49.5 %collective-permute-start.58 = (bf16[2,192,256]{2,1,0:T(8,128)(2,1)}, bf16[2,192,256]{2,1,0:T(8,128)(2,1)}, u32[]{:S(2)}, u32[]{:S(2)}) collective-permute-start(bf16[2,192,256]{2,1,0:T(8,128)(2,1)} %pad_maximum_fusion.16), channel_id=1, source_target_pairs={{0,24},{4,28},{8,0},{12,4},{16,8},{20,12},{24,16},{28,20},{1,25},{... | collective-permute-start | bytes 589832 | tf_op jit(solution)/shard_map/ppermute | solution.py:49
  148.8 42.7 %collective-permute-start.50 = (bf16[4,192,256]{2,1,0:T(8,128)(2,1)}, bf16[4,192,256]{2,1,0:T(8,128)(2,1)}, u32[]{:S(2)}, u32[]{:S(2)}) collective-permute-start(bf16[4,192,256]{2,1,0:T(8,128)(2,1)} %pad_maximum_fusion.7), channel_id=1, source_target_pairs={{0,4},{4,0},{8,12},{12,8},{16,20},{20,16},{24,28},{28,24},{1,5},{5... | collective-permute-start | bytes 1179656 | tf_op jit(solution)/shard_map/ppermute | solution.py:49
  219.5 179.8 %collective-permute-start.53 = (bf16[2,192,256]{2,1,0:T(8,128)(2,1)}, bf16[2,192,256]{2,1,0:T(8,128)(2,1)}, u32[]{:S(2)}, u32[]{:S(2)}) collective-permute-start(bf16[2,192,256]{2,1,0:T(8,128)(2,1)} %pad_maximum_fusion.13), channel_id=1, source_target_pairs={{0,24},{4,28},{8,0},{12,4},{16,8},{20,12},{24,16},{28,20},{1,25},{... | collective-permute-start | bytes 589832 | tf_op jit(solution)/shard_map/ppermute | solution.py:49
  261.3 70.2 %collective-permute-start.43 = (bf16[1,512,256]{2,1,0:T(8,128)(2,1)}, bf16[1,512,256]{2,1,0:T(8,128)(2,1)}, u32[]{:S(2)}, u32[]{:S(2)}) collective-permute-start(bf16[1,512,256]{2,1,0:T(8,128)(2,1)} %get-tuple-element.46.refs_16_), channel_id=1, source_target_pairs={{0,4},{4,0},{8,12},{12,8},{16,20},{20,16},{24,28},{28,24},{1,5},{5... | collective-permute-start | bytes 786440 | tf_op jit(solution)/shard_map/ppermute | solution.py:49
  261.6 143.0 %collective-permute-start.44 = (bf16[1,512,256]{2,1,0:T(8,128)(2,1)}, bf16[1,512,256]{2,1,0:T(8,128)(2,1)}, u32[]{:S(2)}, u32[]{:S(2)}) collective-permute-start(bf16[1,512,256]{2,1,0:T(8,128)(2,1)} %get-tuple-element.46.refs_16_), channel_id=1, source_target_pairs={{0,8},{4,12},{8,16},{12,20},{16,24},{20,28},{24,0},{28,4},{1,9},{5... | collective-permute-start | bytes 786440 | tf_op jit(solution)/shard_map/ppermute | solution.py:49
  331.5 73.2 %collective-permute-start.37 = (bf16[5,512,256]{2,1,0:T(8,128)(2,1)}, bf16[5,512,256]{2,1,0:T(8,128)(2,1)}, u32[]{:S(2)}, u32[]{:S(2)}) collective-permute-start(bf16[5,512,256]{2,1,0:T(8,128)(2,1)} %get-tuple-element.45.refs_8_), channel_id=1, source_target_pairs={{0,8},{4,12},{8,16},{12,20},{16,24},{20,28},{24,0},{28,4},{1,9},{5... | collective-permute-start | bytes 3932168 | tf_op jit(solution)/shard_map/ppermute | solution.py:49
  338.6 66.1 %collective-permute-start.45 = (bf16[1,512,256]{2,1,0:T(8,128)(2,1)}, bf16[1,512,256]{2,1,0:T(8,128)(2,1)}, u32[]{:S(2)}, u32[]{:S(2)}) collective-permute-start(bf16[1,512,256]{2,1,0:T(8,128)(2,1)} %collective-permute-done.43.refs_17_), channel_id=1, source_target_pairs={{0,8},{4,12},{8,16},{12,20},{16,24},{20,28},{24,0},{28,4},{1,9},{5... | collective-permute-start | bytes 786440 | tf_op jit(solution)/shard_map/ppermute | solution.py:49
  340.0 33.4 %collective-permute-start.18 = (bf16[512,128]{1,0:T(8,128)(2,1)S(1)}, bf16[512,128]{1,0:T(8,128)(2,1)S(1)}, u32[]{:S(2)}, u32[]{:S(2)}) collective-permute-start(bf16[512,128]{1,0:T(8,128)(2,1)S(1)} %fusion.34), channel_id=1, source_target_pairs={{0,8},{4,12},{8,16},{12,20},{16,24},{20,28},{24,0},{28,4},{1,9},{5... | collective-permute-start | bytes 393224 | tf_op jit(solution)/shard_map/ppermute | solution.py:49
  404.6 44.6 %collective-permute-start.54 = (bf16[8,192,256]{2,1,0:T(8,128)(2,1)}, bf16[8,192,256]{2,1,0:T(8,128)(2,1)}, u32[]{:S(2)}, u32[]{:S(2)}) collective-permute-start(bf16[8,192,256]{2,1,0:T(8,128)(2,1)} %constant_dynamic-update-slice_fusion), channel_id=1, source_target_pairs={{0,1},{1,0},{2,3},{3,2},{4,5},{5,4},{6,7},{7,6},{8,9},{9,8},{10,11... | collective-permute-start | bytes 2359304 | tf_op jit(solution)/shard_map/ppermute | solution.py:53
  404.8 51.8 %collective-permute-start.46 = (bf16[1,512,256]{2,1,0:T(8,128)(2,1)}, bf16[1,512,256]{2,1,0:T(8,128)(2,1)}, u32[]{:S(2)}, u32[]{:S(2)}) collective-permute-start(bf16[1,512,256]{2,1,0:T(8,128)(2,1)} %collective-permute-done.44.refs_18_), channel_id=1, source_target_pairs={{0,8},{4,12},{8,16},{12,20},{16,24},{20,28},{24,0},{28,4},{1,9},{5... | collective-permute-start | bytes 786440 | tf_op jit(solution)/shard_map/ppermute | solution.py:49
  404.8 51.9 %collective-permute-start.47 = (bf16[1,512,256]{2,1,0:T(8,128)(2,1)}, bf16[1,512,256]{2,1,0:T(8,128)(2,1)}, u32[]{:S(2)}, u32[]{:S(2)}) collective-permute-start(bf16[1,512,256]{2,1,0:T(8,128)(2,1)} %collective-permute-done.45.refs_19_), channel_id=1, source_target_pairs={{0,8},{4,12},{8,16},{12,20},{16,24},{20,28},{24,0},{28,4},{1,9},{5... | collective-permute-start | bytes 786440 | tf_op jit(solution)/shard_map/ppermute | solution.py:49
  404.9 51.7 %collective-permute-start.39 = (bf16[5,512,256]{2,1,0:T(8,128)(2,1)}, bf16[5,512,256]{2,1,0:T(8,128)(2,1)}, u32[]{:S(2)}, u32[]{:S(2)}) collective-permute-start(bf16[5,512,256]{2,1,0:T(8,128)(2,1)} %collective-permute-done.37.refs_10_), channel_id=1, source_target_pairs={{0,8},{4,12},{8,16},{12,20},{16,24},{20,28},{24,0},{28,4},{1,9},{5... | collective-permute-start | bytes 3932168 | tf_op jit(solution)/shard_map/ppermute | solution.py:49
  454.7 53.0 %collective-permute-start.12 = (f32[256,1536]{0,1:T(8,128)}, f32[256,1536]{0,1:T(8,128)}, u32[]{:S(2)}, u32[]{:S(2)}) collective-permute-start(f32[256,1536]{0,1:T(8,128)} %get-tuple-element.116), channel_id=1, source_target_pairs={{0,1},{1,0},{2,3},{3,2},{4,5},{5,4},{6,7},{7,6},{8,9},{9,8},{10,11... | collective-permute-start | bytes 4718600 | tf_op jit(solution)/shard_map/ppermute | solution.py:53
  456.6 49.2 %collective-permute-start.36 = (bf16[5,512,256]{2,1,0:T(8,128)(2,1)}, bf16[5,512,256]{2,1,0:T(8,128)(2,1)}, u32[]{:S(2)}, u32[]{:S(2)}) collective-permute-start(bf16[5,512,256]{2,1,0:T(8,128)(2,1)} %get-tuple-element.45.refs_8_), channel_id=1, source_target_pairs={{0,4},{4,0},{8,12},{12,8},{16,20},{20,16},{24,28},{28,24},{1,5},{5... | collective-permute-start | bytes 3932168 | tf_op jit(solution)/shard_map/ppermute | solution.py:49
  456.6 50.4 %collective-permute-start.41 = (bf16[5,512,256]{2,1,0:T(8,128)(2,1)}, bf16[5,512,256]{2,1,0:T(8,128)(2,1)}, u32[]{:S(2)}, u32[]{:S(2)}) collective-permute-start(bf16[5,512,256]{2,1,0:T(8,128)(2,1)} %collective-permute-done.39.refs_12_), channel_id=1, source_target_pairs={{0,8},{4,12},{8,16},{12,20},{16,24},{20,28},{24,0},{28,4},{1,9},{5... | collective-permute-start | bytes 3932168 | tf_op jit(solution)/shard_map/ppermute | solution.py:49
  456.7 39.3 %collective-permute-start.48 = (bf16[1,512,256]{2,1,0:T(8,128)(2,1)}, bf16[1,512,256]{2,1,0:T(8,128)(2,1)}, u32[]{:S(2)}, u32[]{:S(2)}) collective-permute-start(bf16[1,512,256]{2,1,0:T(8,128)(2,1)} %collective-permute-done.46.refs_20_), channel_id=1, source_target_pairs={{0,8},{4,12},{8,16},{12,20},{16,24},{20,28},{24,0},{28,4},{1,9},{5... | collective-permute-start | bytes 786440 | tf_op jit(solution)/shard_map/ppermute | solution.py:49
  501.5 34.0 %collective-permute-start.38 = (bf16[5,512,256]{2,1,0:T(8,128)(2,1)}, bf16[5,512,256]{2,1,0:T(8,128)(2,1)}, u32[]{:S(2)}, u32[]{:S(2)}) collective-permute-start(bf16[5,512,256]{2,1,0:T(8,128)(2,1)} %collective-permute-done.37.refs_10_), channel_id=1, source_target_pairs={{0,4},{4,0},{8,12},{12,8},{16,20},{20,16},{24,28},{28,24},{1,5},{5... | collective-permute-start | bytes 3932168 | tf_op jit(solution)/shard_map/ppermute | solution.py:49
  505.7 56.2 %collective-permute-start.40 = (bf16[5,512,256]{2,1,0:T(8,128)(2,1)}, bf16[5,512,256]{2,1,0:T(8,128)(2,1)}, u32[]{:S(2)}, u32[]{:S(2)}) collective-permute-start(bf16[5,512,256]{2,1,0:T(8,128)(2,1)} %collective-permute-done.39.refs_12_), channel_id=1, source_target_pairs={{0,4},{4,0},{8,12},{12,8},{16,20},{20,16},{24,28},{28,24},{1,5},{5... | collective-permute-start | bytes 3932168 | tf_op jit(solution)/shard_map/ppermute | solution.py:49
  507.0 82.1 %collective-permute-start.42 = (bf16[5,512,256]{2,1,0:T(8,128)(2,1)}, bf16[5,512,256]{2,1,0:T(8,128)(2,1)}, u32[]{:S(2)}, u32[]{:S(2)}) collective-permute-start(bf16[5,512,256]{2,1,0:T(8,128)(2,1)} %collective-permute-done.41.refs_14_), channel_id=1, source_target_pairs={{0,4},{4,0},{8,12},{12,8},{16,20},{20,16},{24,28},{28,24},{1,5},{5... | collective-permute-start | bytes 3932168 | tf_op jit(solution)/shard_map/ppermute | solution.py:49
  507.8 114.3 %collective-permute-start.26 = (f32[256,1536]{0,1:T(8,128)}, f32[256,1536]{0,1:T(8,128)}, u32[]{:S(2)}, u32[]{:S(2)}) collective-permute-start(f32[256,1536]{0,1:T(8,128)} %fusion.8), channel_id=1, source_target_pairs={{0,1},{1,0},{2,3},{3,2},{4,5},{5,4},{6,7},{7,6},{8,9},{9,8},{10,11... | collective-permute-start | bytes 4718600 | tf_op jit(solution)/shard_map/ppermute | solution.py:53
  533.4 87.3 %collective-permute-start.33 = (bf16[192,768]{0,1:T(8,128)(2,1)}, bf16[192,768]{0,1:T(8,128)(2,1)}, u32[]{:S(2)}, u32[]{:S(2)}) collective-permute-start(bf16[192,768]{0,1:T(8,128)(2,1)} %add_convert_fusion.4), channel_id=1, source_target_pairs={{0,8},{4,12},{8,16},{12,20},{16,24},{20,28},{24,0},{28,4},{1,9},{5... | collective-permute-start | bytes 884744 | tf_op jit(solution)/shard_map/ppermute | solution.py:49
  (92 other events, 1267.6 us)

commit v2 on v1

v2 whole, which is shorter than its diff:
```python
import functools

import jax
import jax.numpy as jnp
from jax import lax
from jax.experimental import pallas as pl
from jax.experimental.pallas import tpu as pltpu
from jax.sharding import PartitionSpec as P

H = 24
KV = 8
HD = 64
eps = 1e-05
NEG = -1e30
F32 = jnp.float32
BF = jnp.bfloat16
VLIM = 60 * 1024 * 1024
EXTRA = 16
NT = (((1,), (1,)), ((), ()))
TN = (((0,), (0,)), ((), ()))


def digits_of(n):
    out = []
    stride = 1
    while n > 1:
        if stride == 1 and n % 2 == 0:
            radix = 2
        elif n % 4 == 0:
            radix = 4
        else:
            radix = n
        out.append((stride, radix))
        stride *= radix
        n //= radix
    return out


def moved(n, digit, shift):
    stride, radix = digit
    pairs = []
    for i in range(n):
        d = (i // stride) % radix
        pairs.append((i, i + ((d + shift) % radix - d) * stride))
    return pairs


def hop(x, n, digit, shift=1):
    return lax.ppermute(x, "ctx", moved(n, digit, shift))


def other_core(x):
    return lax.ppermute(x, "wa", [(i, i ^ 1) for i in range(4)])


def other_chip(x):
    return lax.ppermute(x, "wa", [(i, i ^ 2) for i in range(4)])


def rel_keys(digits):
    keys = [()]
    for _, radix in digits:
        keys = [k + (r,) for r in range(radix) for k in keys]
    return keys


def set_digit(key, at, value):
    return key[:at] + (value,) + key[at + 1 :]


def gather_ctx(x, n, digits, order):
    blocks = {tuple(0 for _ in digits): x}
    for at in order:
        fresh = {}
        for key, block in blocks.items():
            moving = block
            for s in range(1, digits[at][1]):
                moving = hop(moving, n, digits[at])
                fresh[set_digit(key, at, s)] = moving
        blocks.update(fresh)
    return blocks


def scatter_ctx(stack, n, order, add, hold=lambda at, x: x):
    moving = stack
    hops = 0
    for at in reversed(range(len(order))):
        radix = order[at][1]
        if isinstance(moving, (list, tuple)):
            blocks = moving
        else:
            per = moving.shape[0] // radix
            blocks = [moving[r * per : (r + 1) * per] for r in range(radix)]
        moving = blocks[1]
        for s in range(2, radix + 1):
            moving = hold(hops, hop(moving, n, order[at]))
            moving = add(moving, blocks[s % radix])
            hops += 1
    return moving[0]


def add_bf(a, b):
    return (a.astype(F32) + b.astype(F32)).astype(BF)


def stack_kernel(places, *refs):
    for i, (at, unit) in enumerate(places):
        refs[-1][i] = refs[at][unit]


def stacked(pieces):
    arrays = []
    places = []
    for array, unit in pieces:
        at = next((i for i, x in enumerate(arrays) if x is array), None)
        if at is None:
            at = len(arrays)
            arrays.append(array)
        places.append((at, unit))
    shape = (len(pieces),) + arrays[0].shape[1:]
    return pl.pallas_call(
        functools.partial(stack_kernel, tuple(places)),
        out_shape=jax.ShapeDtypeStruct(shape, arrays[0].dtype),
        in_specs=vspec(len(arrays)),
        out_specs=vspec(1)[0],
        compiler_params=params(),
        name="stacked",
        cost_estimate=cost(1),
    )(*arrays)


def exchange_top(groups, n, digits):
    return [groups[0]] + [hop(groups[r], n, digits[-1], r) for r in range(1, len(groups))]


def exchange_rest(groups, n, digits):
    keys = rel_keys(digits)
    per = n // len(groups)
    parts = {i: (groups[i // per], i % per) for i in range(n)}
    for at in reversed(range(len(digits) - 1)):
        for s in range(1, digits[at][1]):
            chosen = [i for i, k in enumerate(keys) if k[at] == s]
            bundle = hop(stacked([parts[i] for i in chosen]), n, digits[at], s)
            for place, i in enumerate(chosen):
                parts[i] = (bundle, place)
    return [parts[i] for i in range(n)]


def swapped(pieces, first):
    arrays = []
    for array, _ in pieces:
        if not any(array is x for x in arrays):
            arrays.append(array)
    held = tie(arrays, first)
    pieces = [(held[next(i for i, x in enumerate(arrays) if x is a)], u) for a, u in pieces]
    near = stacked(pieces)
    return near, other_core(near)


def digit_offset(me, key, digits, sign):
    place = 0
    for (stride, radix), r in zip(digits, key):
        d = (me // stride) % radix
        place = place + ((d + sign * r) % radix) * stride
    return place


def tie_kernel(*refs):
    pass


def tie(xs, first):
    xs, first = list(xs), list(first)
    return pl.pallas_call(
        tie_kernel,
        out_shape=tuple(jax.ShapeDtypeStruct(x.shape, x.dtype) for x in xs),
        in_specs=anywhere(len(xs) + len(first)),
        out_specs=tuple(anywhere(len(xs))),
        input_output_aliases={i: i for i in range(len(xs))},
        name="tie",
    )(*xs, *first)


def diagonal(x):
    return lax.ppermute(x, "wa", [(i, i ^ 3) for i in range(4)])


def all_parts(near, far):
    return [near, other_core(far), other_chip(near), diagonal(far)]


def cost(us):
    return pl.CostEstimate(flops=int(us * 1e9), bytes_accessed=int(us * 3e6), transcendentals=0)


def params(**kw):
    return pltpu.CompilerParams(vmem_limit_bytes=VLIM, **kw)


def vspec(n):
    return [pl.BlockSpec(memory_space=pltpu.VMEM)] * n


def drop_first(kernel, at, count):
    if not count:
        return kernel

    def waiting(*refs):
        kernel(*refs[:at], *refs[at + count :])

    return waiting


def anywhere(count):
    return [pl.BlockSpec(memory_space=pl.ANY)] * count


def project_kernel(core_ref, x_ref, gain_ref, wq_ref, wk_ref, wv_ref, extra_ref, a1_ref, q_ref, kv_ref):
    tok = x_ref.shape[0]
    half = tok // 2
    kvw = wk_ref.shape[1]
    for i in range(2):
        start = pl.multiple_of(((core_ref[0] + i) % 2) * half, half)
        x = x_ref[pl.ds(start, half), :].astype(F32)
        inv = lax.rsqrt(jnp.mean(x * x, axis=-1, keepdims=True) + eps)
        a1 = (x * inv * gain_ref[...][None, :]).astype(BF)
        rows = pl.ds(i * half, half)
        a1_ref[rows, :] = a1
        kv_ref[rows, :kvw] = jnp.dot(a1, wk_ref[...], preferred_element_type=F32).astype(BF)
        kv_ref[rows, kvw:] = jnp.dot(a1, wv_ref[...], preferred_element_type=F32).astype(BF)
        q = jnp.dot(a1, wq_ref[...], preferred_element_type=F32).astype(BF)
        q_ref[rows, :] = (q.astype(F32) * HD ** (-0.5)).astype(BF)
    kv_ref[pl.ds(tok, EXTRA), :] = extra_ref[...]


def project(core, x, gain, wq, wk, wv, extra):
    tok, width = x.shape
    return pl.pallas_call(
        project_kernel,
        out_shape=(
            jax.ShapeDtypeStruct((tok, width), BF),
            jax.ShapeDtypeStruct((tok, wq.shape[1]), BF),
            jax.ShapeDtypeStruct((tok + EXTRA, 2 * wk.shape[1]), BF),
        ),
        in_specs=[pl.BlockSpec(memory_space=pltpu.SMEM)] + vspec(6),
        out_specs=tuple(vspec(3)),
        compiler_params=params(),
        name="project",
        cost_estimate=cost(5),
    )(core, x, gain, wq, wk, wv, extra)


def seg_onehot(row):
    lane = lax.broadcasted_iota(jnp.int32, (16, row.shape[1]), 0).astype(F32)
    return jnp.where(lane == row, 1.0, 0.0).astype(BF)


def seg_rows_of(block, tok):
    width = block.shape[1]
    return [
        block[tok : tok + EXTRA, :].astype(F32)[i : i + 1, :] for i in range(tok // width)
    ]


def attend_kernel(nb, heads, groups, *refs):
    q_ref = refs[0]
    kv_refs = refs[1 : 1 + nb]
    hf_ref, near_ref, far_ref, lse_ref = refs[1 + nb : 5 + nb]
    kv_s, q_s, m_s, l_s, acc_s = refs[5 + nb :]
    tok = q_ref.shape[0]
    kvw = kv_refs[0].shape[1] // 2
    for b in range(nb):
        kv_s[b] = kv_refs[b][...]
    for h in range(heads):
        q_s[h] = q_ref[:, h * HD : (h + 1) * HD]
    own = jnp.concatenate(seg_rows_of(kv_s[0], tok), axis=1)
    own_hot = seg_onehot(own)
    own_lo = jnp.min(own)
    own_hi = jnp.max(own)
    m_s[...] = jnp.full(m_s.shape, NEG, F32)
    l_s[...] = jnp.zeros(l_s.shape, F32)
    acc_s[...] = jnp.zeros(acc_s.shape, F32)

    def body(b, masked):
        block = kv_s[b]
        if masked:
            seg = jnp.concatenate(seg_rows_of(block, tok), axis=1)
            same = lax.dot_general(seg_onehot(seg), own_hot, TN, preferred_element_type=F32) > 0.5
        for n in range(heads // groups):
            k = block[:tok, n * HD : (n + 1) * HD]
            v = block[:tok, kvw + n * HD : kvw + (n + 1) * HD]
            for h in range(n * groups, (n + 1) * groups):
                s = lax.dot_general(k, q_s[h], NT, preferred_element_type=F32)
                if masked:
                    s = jnp.where(same, s, NEG)
                m_old = m_s[h : h + 1, :]
                m_new = jnp.maximum(m_old, jnp.max(s, axis=0, keepdims=True))
                p = jnp.exp(s - m_new)
                f = jnp.exp(m_old - m_new)
                m_s[h : h + 1, :] = m_new
                l_s[h : h + 1, :] = l_s[h : h + 1, :] * f + jnp.sum(p, axis=0, keepdims=True)
                acc_s[h] = acc_s[h] * f + lax.dot_general(
                    v, p.astype(BF), TN, preferred_element_type=F32
                )

    def visit(b, carry):
        seg = jnp.concatenate(seg_rows_of(kv_s[b], tok), axis=1)
        lo = jnp.min(seg)
        hi = jnp.max(seg)
        plain = (lo == hi) & (own_lo == own_hi) & (lo == own_lo)
        touch = (lo <= own_hi) & (own_lo <= hi)

        @pl.when(plain)
        def _():
            body(b, False)

        @pl.when(touch & jnp.logical_not(plain))
        def _():
            body(b, True)

        return carry

    lax.fori_loop(0, nb, visit, 0)
    rows = []
    for h in range(heads):
        rows.append(acc_s[h] / l_s[h : h + 1, :])
        lse_ref[h : h + 1, :] = m_s[h : h + 1, :] + jnp.log(l_s[h : h + 1, :])
    out = jnp.concatenate(rows, axis=0).T
    hf_ref[...] = out
    near_ref[...] = out[: tok // 2].astype(BF)
    far_ref[...] = out[tok // 2 :].astype(BF)


def attend(q, blocks, heads, groups, first=()):
    tok = q.shape[0]
    nb = len(blocks)
    return pl.pallas_call(
        drop_first(functools.partial(attend_kernel, nb, heads, groups), 1 + nb, len(first)),
        out_shape=(
            jax.ShapeDtypeStruct((tok, heads * HD), F32),
            jax.ShapeDtypeStruct((tok // 2, heads * HD), BF),
            jax.ShapeDtypeStruct((tok // 2, heads * HD), BF),
            jax.ShapeDtypeStruct((8, tok), F32),
        ),
        in_specs=vspec(1 + nb) + anywhere(len(first)),
        out_specs=tuple(vspec(4)),
        scratch_shapes=[
            pltpu.VMEM((nb,) + blocks[0].shape, BF),
            pltpu.VMEM((heads, tok, HD), BF),
            pltpu.VMEM((8, tok), F32),
            pltpu.VMEM((8, tok), F32),
            pltpu.VMEM((heads, HD, tok), F32),
        ],
        compiler_params=params(),
        name="attend",
        cost_estimate=cost(27),
    )(q, *blocks, *first)


def attend_back_kernel(pairs, heads, groups, start, end, *refs):
    q_ref, own_ref, lse_ref = refs[:3]
    nb = 2 * pairs
    kv_refs = refs[3 : 3 + nb]
    at = 3 + nb
    if start:
        att_near_ref, att_far_ref, wo_ref, hf_ref = refs[at : at + 4]
        at += 4
    else:
        grad_in_ref, delta_in_ref, dq_in_ref = refs[at : at + 3]
        at += 3
    dkv_refs = refs[at : at + pairs]
    at += pairs
    if start:
        grad_ref, delta_ref = refs[at : at + 2]
        at += 2
    if end:
        dq_near_ref, dq_far_ref = refs[at : at + 2]
        at += 2
    else:
        dq_out_ref = refs[at]
        at += 1
    kv_s, q_s, do_s, delta_s, dq_s, dkv_s = refs[at:]
    tok = q_ref.shape[0]
    kvw = own_ref.shape[1] // 2
    if start:
        grad = jnp.concatenate(
            [
                lax.dot_general(ref[...], wo_ref[...], NT, preferred_element_type=F32)
                for ref in (att_near_ref, att_far_ref)
            ],
            axis=0,
        ).astype(BF)
        grad_ref[...] = grad
        prod = (grad.astype(F32) * hf_ref[...]).T
        for h in range(heads):
            delta_s[h : h + 1, :] = jnp.sum(prod[h * HD : (h + 1) * HD, :], axis=0, keepdims=True)
        delta_ref[...] = delta_s[...]
        dq_s[...] = jnp.zeros(dq_s.shape, F32)
    else:
        grad = grad_in_ref[...]
        delta_s[...] = delta_in_ref[...]
        dq_s[...] = dq_in_ref[...]
    for b in range(nb):
        kv_s[b] = kv_refs[b][...]
    for h in range(heads):
        q_s[h] = q_ref[:, h * HD : (h + 1) * HD]
        do_s[h] = grad[:, h * HD : (h + 1) * HD]
    own = jnp.concatenate(seg_rows_of(own_ref, tok), axis=1)
    own_hot = seg_onehot(own)
    own_lo = jnp.min(own)
    own_hi = jnp.max(own)

    def body(b, masked):
        block = kv_s[b]
        if masked:
            seg = jnp.concatenate(seg_rows_of(block, tok), axis=1)
            same = lax.dot_general(seg_onehot(seg), own_hot, TN, preferred_element_type=F32) > 0.5
        for n in range(heads // groups):
            k = block[:tok, n * HD : (n + 1) * HD]
            v = block[:tok, kvw + n * HD : kvw + (n + 1) * HD]
            dk = None
            for h in range(n * groups, (n + 1) * groups):
                s = lax.dot_general(k, q_s[h], NT, preferred_element_type=F32)
                p = jnp.exp(s - lse_ref[h : h + 1, :])
                if masked:
                    p = jnp.where(same, p, 0.0)
                dv_h = jnp.dot(p.astype(BF), do_s[h], preferred_element_type=F32)
                dp = lax.dot_general(v, do_s[h], NT, preferred_element_type=F32)
                ds = (p * (dp - delta_s[h : h + 1, :])).astype(BF)
                dk_h = jnp.dot(ds, q_s[h], preferred_element_type=F32)
                dq_s[h] += lax.dot_general(k, ds, TN, preferred_element_type=F32)
                dk = dk_h if dk is None else dk + dk_h
                dv = dv_h if h == n * groups else dv + dv_h
            dkv_s[b, :, n * HD : (n + 1) * HD] = dk.astype(BF)
            dkv_s[b, :, kvw + n * HD : kvw + (n + 1) * HD] = dv.astype(BF)

    def visit(b, carry):
        seg = jnp.concatenate(seg_rows_of(kv_s[b], tok), axis=1)
        lo = jnp.min(seg)
        hi = jnp.max(seg)
        plain = (lo == hi) & (own_lo == own_hi) & (lo == own_lo)
        touch = (lo <= own_hi) & (own_lo <= hi)

        @pl.when(plain)
        def _():
            body(b, False)

        @pl.when(touch & jnp.logical_not(plain))
        def _():
            body(b, True)

        @pl.when(jnp.logical_not(touch))
        def _():
            dkv_s[b] = jnp.zeros(dkv_s.shape[1:], BF)

        return carry

    lax.fori_loop(0, nb, visit, 0)
    for i in range(pairs):
        dkv_refs[i][...] = dkv_s[2 * i : 2 * i + 2]
    if end:
        out = jnp.concatenate([dq_s[h] for h in range(heads)], axis=0).T
        out = (out * HD ** (-0.5)).astype(BF)
        dq_near_ref[...] = out[: tok // 2]
        dq_far_ref[...] = out[tok // 2 :]
    else:
        dq_out_ref[...] = dq_s[...]


def attend_back(q, own, lse, blocks, heads, groups, start=None, going=None, end=True, first=()):
    tok = q.shape[0]
    nb = len(blocks)
    pairs = nb // 2
    width = heads * HD
    operands = [q, own, lse] + list(blocks) + list(start if start is not None else going)
    outs = [((2, tok, own.shape[1]), BF)] * pairs
    if start is not None:
        outs += [((tok, width), BF), ((8, tok), F32)]
    outs += [((tok // 2, width), BF)] * 2 if end else [((heads, HD, tok), F32)]
    kernel = functools.partial(
        attend_back_kernel, pairs, heads, groups, start is not None, end
    )
    return pl.pallas_call(
        drop_first(kernel, len(operands), len(first)),
        out_shape=tuple(jax.ShapeDtypeStruct(shape, dtype) for shape, dtype in outs),
        in_specs=vspec(len(operands)) + anywhere(len(first)),
        out_specs=tuple(vspec(len(outs))),
        scratch_shapes=[
            pltpu.VMEM((nb,) + blocks[0].shape, BF),
            pltpu.VMEM((heads, tok, HD), BF),
            pltpu.VMEM((heads, tok, HD), BF),
            pltpu.VMEM((8, tok), F32),
            pltpu.VMEM((heads, HD, tok), F32),
            pltpu.VMEM((nb, tok, own.shape[1]), BF),
        ],
        compiler_params=params(),
        name="attend_back",
        cost_estimate=cost(4.5 * nb),
    )(*operands, *first)


def experts_kernel(
    core_ref,
    ids_ref,
    mine_ref,
    theirs_ref,
    g_ref,
    wr_ref,
    wg_ref,
    wu_ref,
    wd_ref,
    mix_keep_ref,
    mix_send_ref,
    dx_keep_ref,
    dx_send_ref,
    gates_ref,
    ent_ref,
    a2_s,
    g_s,
    mix_s,
    dx_s,
    back_s,
):
    e = pl.program_id(0)
    tok, width = a2_s.shape
    half = tok // 2
    experts = wr_ref.shape[0]
    lane = lax.broadcasted_iota(jnp.int32, (tok, experts), 1)
    first = ids_ref[:, 0:1]
    second = ids_ref[:, 1:2]

    @pl.when(e == 0)
    def _():
        a2_s[:half, :] = mine_ref[...]
        a2_s[half:, :] = theirs_ref[...]
        for i in range(2):
            start = pl.multiple_of(((core_ref[0] + i) % 2) * half, half)
            g_s[pl.ds(i * half, half), :] = g_ref[pl.ds(start, half), :]
        logits = lax.dot_general(a2_s[...], wr_ref[...], NT, preferred_element_type=F32)
        one = jnp.sum(jnp.where(lane == first, logits, 0.0), axis=1, keepdims=True)
        two = jnp.sum(jnp.where(lane == second, logits, 0.0), axis=1, keepdims=True)
        top = jnp.maximum(one, two)
        one = jnp.exp(one - top)
        two = jnp.exp(two - top)
        total = one + two
        gates_ref[...] = jnp.where(lane == first, one / total, 0.0) + jnp.where(
            lane == second, two / total, 0.0
        )
        mix_s[...] = jnp.zeros(mix_s.shape, F32)
        dx_s[...] = jnp.zeros(dx_s.shape, F32)
        back_s[...] = jnp.zeros(back_s.shape, F32)
        ent_ref[...] = jnp.zeros(ent_ref.shape, BF)

    wg = wg_ref[0]
    wu = wu_ref[0]
    wd = wd_ref[0]
    for i in range(2):
        rows = pl.ds(i * half, half)
        a2 = a2_s[rows, :]
        u = jnp.dot(a2, wg, preferred_element_type=F32)
        w = jnp.dot(a2, wu, preferred_element_type=F32)
        m = lax.dot_general(g_s[rows, :], wd, NT, preferred_element_type=F32)
        here = lane[:half] == e
        gate = jnp.sum(jnp.where(here, gates_ref[rows, :], 0.0), axis=1, keepdims=True)
        pick_one = (ids_ref[rows, 0:1] == e).astype(F32)
        pick_two = (ids_ref[rows, 1:2] == e).astype(F32)
        sig = 1.0 / (1.0 + jnp.exp(-u))
        act = u * sig
        mid = (act * w).astype(BF).astype(F32)
        back = jnp.sum(mid * m, axis=1, keepdims=True) * (pick_one + pick_two)
        back_s[rows, :] += jnp.where(here, back, 0.0)
        mid = mid * gate
        gm = gate * m
        up_back = gm * act
        pre_back = gm * w * sig * (1.0 + u * (1.0 - sig))
        mid_b = mid.astype(BF)
        up_b = up_back.astype(BF)
        pre_b = pre_back.astype(BF)
        mix_s[rows, :] += jnp.dot(mid_b, wd, preferred_element_type=F32)
        dx_s[rows, :] += lax.dot_general(
            pre_b, wg, NT, preferred_element_type=F32
        ) + lax.dot_general(up_b, wu, NT, preferred_element_type=F32)
        for kind, value in enumerate((mid, pre_back, up_back)):
            for c, pick in enumerate((pick_one, pick_two)):
                ent_ref[2 * kind + c, rows, :] += (value * pick).astype(BF)

    @pl.when(e == pl.num_programs(0) - 1)
    def _():
        mix_keep_ref[...] = mix_s[:half, :]
        mix_send_ref[...] = mix_s[half:, :].astype(BF)
        dx_keep_ref[:, :width] = dx_s[:half, :]
        dx_send_ref[:, :width] = dx_s[half:, :].astype(BF)
        pad = jnp.zeros((half, 128 - experts), F32)
        dx_keep_ref[:, width:] = jnp.concatenate([back_s[:half, :], pad], axis=1)
        dx_send_ref[:, width:] = jnp.concatenate([back_s[half:, :], pad], axis=1).astype(BF)


def experts_call(core, ids, mine, theirs, g, wr, wg, wu, wd, first=()):
    half, width = mine.shape
    tok = 2 * half
    experts, _, hidden = wg.shape

    def whole(*shape):
        return pl.BlockSpec(shape, lambda e, *_: (0,) * len(shape))

    def one(*shape):
        return pl.BlockSpec((1,) + shape, lambda e, *_: (e,) + (0,) * len(shape))

    return pl.pallas_call(
        drop_first(experts_kernel, 9, len(first)),
        out_shape=(
            jax.ShapeDtypeStruct((half, width), F32),
            jax.ShapeDtypeStruct((half, width), BF),
            jax.ShapeDtypeStruct((half, width + 128), F32),
            jax.ShapeDtypeStruct((half, width + 128), BF),
            jax.ShapeDtypeStruct((tok, experts), F32),
            jax.ShapeDtypeStruct((6, tok, hidden), BF),
        ),
        grid=(experts,),
        in_specs=[
            pl.BlockSpec(memory_space=pltpu.SMEM),
            whole(tok, 2),
            whole(half, width),
            whole(half, width),
            whole(tok, width),
            whole(experts, width),
            one(width, hidden),
            one(width, hidden),
            one(hidden, width),
        ]
        + anywhere(len(first)),
        out_specs=(
            whole(half, width),
            whole(half, width),
            whole(half, width + 128),
            whole(half, width + 128),
            whole(tok, experts),
            whole(6, tok, hidden),
        ),
        scratch_shapes=[
            pltpu.VMEM((tok, width), BF),
            pltpu.VMEM((tok, width), BF),
            pltpu.VMEM((tok, width), F32),
            pltpu.VMEM((tok, width), F32),
            pltpu.VMEM((tok, experts), F32),
        ],
        compiler_params=params(dimension_semantics=("arbitrary",)),
        name="experts",
        cost_estimate=cost(32),
    )(core, ids, mine, theirs, g, wr, wg, wu, wd, *first)


def expert_grads_kernel(at, count, seeded, ids_ref, *refs):
    x_refs = refs[0:2]
    g_refs = refs[2:4]
    ents = refs[4 : 4 + count]
    prev = refs[4 + count : 7 + count] if seeded else None
    outs = refs[-3:]
    e = pl.program_id(0)
    sums = [None, None, None]
    for b in range(count):
        half = x_refs[0].shape[2]
        hidden = ents[b].shape[2]
        for i in range(2):
            rows = pl.ds(i * half, half)
            one = jnp.where(ids_ref[at + b, rows, 0:1] == e, 1.0, 0.0).astype(BF)
            two = jnp.where(ids_ref[at + b, rows, 1:2] == e, 1.0, 0.0).astype(BF)
            one = jnp.broadcast_to(one, (half, hidden))
            two = jnp.broadcast_to(two, (half, hidden))
            xt = x_refs[i][at + b]
            gt = g_refs[i][at + b]
            for kind in range(3):
                value = ents[b][2 * kind, rows, :] * one + ents[b][2 * kind + 1, rows, :] * two
                term = jnp.dot(gt if kind == 0 else xt, value, preferred_element_type=F32)
                sums[kind] = term if sums[kind] is None else sums[kind] + term
    for kind in range(3):
        outs[kind][0] = sums[kind] + prev[kind][0] if seeded else sums[kind]


def expert_grads(at, ids, xm, xo, gm, go, ents, experts, prev=None):
    cols = xm.shape[1]
    hidden = ents[0].shape[-1]
    operands = [ids, xm, xo, gm, go] + list(ents)
    specs = [pl.BlockSpec(x.shape, lambda e, nd=x.ndim: (0,) * nd) for x in operands]
    out_spec = pl.BlockSpec((1, cols, hidden), lambda e: (e, 0, 0))
    if prev is not None:
        operands += list(prev)
        specs += [out_spec] * 3
    return pl.pallas_call(
        functools.partial(expert_grads_kernel, at, len(ents), prev is not None),
        out_shape=(jax.ShapeDtypeStruct((experts, cols, hidden), F32),) * 3,
        grid=(experts,),
        in_specs=specs,
        out_specs=(out_spec,) * 3,
        compiler_params=params(dimension_semantics=("arbitrary",)),
        name="expert_grads",
        cost_estimate=cost(3.5 * len(ents)),
    )(*operands)


def my_rows(core_ref, ref):
    half = ref.shape[0] // 2
    return ref[pl.ds(pl.multiple_of(core_ref[0] * half, half), half), :]


def simple(kernel, name, outs, core, *operands, first=()):
    return pl.pallas_call(
        drop_first(kernel, 1 + len(operands), len(first)),
        out_shape=tuple(jax.ShapeDtypeStruct(shape, dtype) for shape, dtype in outs),
        in_specs=[pl.BlockSpec(memory_space=pltpu.SMEM)] + vspec(len(operands)) + anywhere(len(first)),
        out_specs=tuple(vspec(len(outs))),
        compiler_params=params(),
        name=name,
        cost_estimate=cost(5),
    )(core, *operands, *first)


def middle_kernel(core_ref, x_ref, gain_ref, *refs):
    parts, weights = refs[:4], refs[4:8]
    hidden_ref, a2_ref = refs[8:]
    total = my_rows(core_ref, x_ref).astype(F32)
    for part, weight in zip(parts, weights):
        total = total + jnp.dot(part[...], weight[...], preferred_element_type=F32)
    inv = lax.rsqrt(jnp.mean(total * total, axis=-1, keepdims=True) + eps)
    hidden_ref[...] = total
    a2_ref[...] = (total * inv * gain_ref[...][None, :]).astype(BF)


def back_kernel(
    core_ref,
    near_ref,
    got_ref,
    hidden_ref,
    a2_ref,
    gates_ref,
    ids_ref,
    wr_ref,
    gain_ref,
    g_ref,
    grad_ref,
    att_ref,
    misc_ref,
):
    half, width = hidden_ref.shape
    experts = wr_ref.shape[0]
    total = near_ref[...].astype(F32) + got_ref[...].astype(F32)
    gate_back = total[:, width:][:, :experts]
    gates = gates_ref[:half, :]
    lane = lax.broadcasted_iota(jnp.int32, (half, experts), 1)
    picked = (lane == ids_ref[:half, 0:1]) | (lane == ids_ref[:half, 1:2])
    logit = gates * (gate_back - jnp.sum(gates * gate_back, axis=-1, keepdims=True))
    logit = jnp.where(picked, logit, 0.0).astype(BF)
    back = total[:, :width] + jnp.dot(logit, wr_ref[...], preferred_element_type=F32)
    hidden = hidden_ref[...]
    inv = lax.rsqrt(jnp.mean(hidden * hidden, axis=-1, keepdims=True) + eps)
    upstream = my_rows(core_ref, g_ref).astype(F32)
    scaled = back * gain_ref[...][None, :]
    grad = upstream + inv * (
        scaled - hidden * inv * inv * jnp.mean(scaled * hidden, axis=-1, keepdims=True)
    )
    grad_ref[...] = grad
    att_ref[...] = grad.astype(BF)
    misc_ref[:8, :] = lax.dot_general(logit, a2_ref[...], TN, preferred_element_type=F32)
    ffn = jnp.sum(back * hidden * inv, axis=0, keepdims=True)
    misc_ref[8:, :] = jnp.broadcast_to(ffn, (8, width))


def query_back_kernel(core_ref, *refs):
    parts, weights, out_ref = refs[:4], refs[4:8], refs[8]
    total = None
    for part, weight in zip(parts, weights):
        term = lax.dot_general(
            part[...], weight[:, : part.shape[1]], NT, preferred_element_type=F32
        )
        total = term if total is None else total + term
    out_ref[...] = total


def input_kernel(core_ref, x_ref, gain_ref, grad_ref, query_ref, *refs):
    parts, weights = refs[:4], refs[4:8]
    out_ref, norm_ref = refs[8:]
    back = query_ref[...]
    for part, weight in zip(parts, weights):
        start = weight.shape[1] - part.shape[1]
        back = back + lax.dot_general(
            part[...], weight[:, start:], NT, preferred_element_type=F32
        )
    x = my_rows(core_ref, x_ref).astype(F32)
    inv = lax.rsqrt(jnp.mean(x * x, axis=-1, keepdims=True) + eps)
    scaled = back * gain_ref[...][None, :]
    out_ref[...] = grad_ref[...] + inv * (
        scaled - x * inv * inv * jnp.mean(scaled * x, axis=-1, keepdims=True)
    )
    norm = jnp.sum(back * x * inv, axis=0, keepdims=True)
    norm_ref[...] = jnp.broadcast_to(norm, norm_ref.shape)


def place_kernel(core_ref, mine_ref, theirs_ref, out_ref):
    half = mine_ref.shape[0]
    out_ref[pl.ds(pl.multiple_of(core_ref[0] * half, half), half), :] = mine_ref[...]
    out_ref[pl.ds(pl.multiple_of((1 - core_ref[0]) * half, half), half), :] = theirs_ref[...]


def columns_kernel(waits, owner_ref, core_ref, x_ref, *refs):
    outs, turned = refs[waits:-1], refs[-1]
    per, cols, half = outs[0].shape
    x = my_rows(core_ref, x_ref) if x_ref.shape[0] != half else x_ref[...]
    turned[...] = x.T
    for r, out_ref in enumerate(outs):
        for i in range(per):
            rows = pl.ds(pl.multiple_of(owner_ref[r * per + i] * cols, 16), cols)
            out_ref[i] = turned[rows, :]


def columns(owner, core, x, half, groups, first=()):
    n = owner.shape[0]
    width = x.shape[1]
    smem = pl.BlockSpec(memory_space=pltpu.SMEM)
    out = jax.ShapeDtypeStruct((n // groups, width // n, half), BF)
    return pl.pallas_call(
        functools.partial(columns_kernel, len(first)),
        out_shape=(out,) * groups,
        in_specs=[smem, smem] + vspec(1) + [pl.BlockSpec(memory_space=pl.ANY)] * len(first),
        out_specs=tuple(vspec(groups)),
        scratch_shapes=[pltpu.VMEM((width, half), BF)],
        compiler_params=params(),
        name="columns",
        cost_estimate=cost(2.5),
    )(owner, core, x, *first)


def weight_kernel(shape, extra, owner_ref, *refs):
    out_ref, turned, misc_turned = refs[-3:]
    n, cols, _ = out_ref.shape
    at = 0
    column = 0
    for group, pairs in enumerate(shape):
        lefts, rights = refs[at : at + pairs], refs[at + pairs : at + 2 * pairs]
        at += 2 * pairs
        row = 0
        for left in lefts:
            turned[group, :, row : row + left.shape[0]] = left[...].T
            row += left.shape[0]
        right = jnp.concatenate([r[...] for r in rights], axis=0) if pairs > 1 else rights[0][...]
        for i in range(n):
            rows = pl.ds(pl.multiple_of(owner_ref[i] * cols, 16), cols)
            out_ref[i, :, column : column + right.shape[1]] = jnp.dot(
                turned[group, rows, :], right, preferred_element_type=F32
            ).astype(BF)
        column += right.shape[1]
    if extra:
        misc = refs[at][...]
        spare = jnp.zeros((128 - misc.shape[0], misc.shape[1]), F32)
        misc_turned[...] = jnp.concatenate([misc, spare], axis=0).T
        for i in range(n):
            rows = pl.ds(pl.multiple_of(owner_ref[i] * cols, 16), cols)
            out_ref[i, :, column:] = misc_turned[rows, :].astype(BF)


def weight_terms(owner, groups, misc=None, us=4, first=()):
    n = owner.shape[0]
    width = groups[0][0][0].shape[1]
    rows = sum(x.shape[0] for x in groups[0][0])
    out_width = sum(rights[0].shape[1] for _, rights in groups)
    operands = []
    for lefts, rights in groups:
        operands += list(lefts) + list(rights)
    if misc is not None:
        operands.append(misc)
        out_width += 128
    shape = tuple(len(lefts) for lefts, _ in groups)
    return pl.pallas_call(
        drop_first(
            functools.partial(weight_kernel, shape, misc is not None),
            1 + len(operands),
            len(first),
        ),
        out_shape=jax.ShapeDtypeStruct((n, width // n, out_width), BF),
        in_specs=[pl.BlockSpec(memory_space=pltpu.SMEM)]
        + vspec(len(operands))
        + anywhere(len(first)),
        out_specs=vspec(1)[0],
        scratch_shapes=[pltpu.VMEM((len(groups), width, rows), BF), pltpu.VMEM((width, 128), F32)],
        compiler_params=params(),
        name="weight_terms",
        cost_estimate=cost(us),
    )(owner, *operands, *first)


def per_device(
    n_ctx,
    layer_input,
    segment_ids,
    expert_ids,
    norm_gain,
    query_weight,
    key_weight,
    value_weight,
    output_weight,
    ffn_gain,
    router_weight,
    gate_weight,
    up_weight,
    down_weight,
    cotangent,
):
    tok, width = layer_input.shape
    half = tok // 2
    groups = H // KV
    kv_local = key_weight.shape[1] // HD
    heads = kv_local * groups
    kvw = key_weight.shape[1]
    experts = gate_weight.shape[0]
    cols = width // n_ctx
    digits = digits_of(n_ctx)
    keys = rel_keys(digits)
    upper_first = list(range(1, len(digits))) + [0]
    lower_first = list(range(len(digits)))
    me = lax.axis_index("ctx")
    core = lax.axis_index("wa") % 2
    core_arr = jnp.full((1,), core, jnp.int32)
    owner_to = jnp.stack([digit_offset(me, k, digits, 1) for k in keys]).astype(jnp.int32)
    owner_from = jnp.stack([digit_offset(me, k, digits, -1) for k in keys]).astype(jnp.int32)
    gain_one, gain_two = norm_gain, ffn_gain
    router = router_weight.T

    def mine_first(x):
        return jnp.where(core == 0, x, jnp.concatenate([x[half:], x[:half]], axis=0))

    segs = mine_first(segment_ids).astype(BF)
    ids = mine_first(expert_ids)
    extra = jnp.concatenate([segs, ids[:, 0].astype(BF), ids[:, 1].astype(BF)])
    extra = jnp.pad(extra, (0, EXTRA * 2 * kvw - extra.shape[0])).reshape(EXTRA, 2 * kvw)
    a1, q, kv = project(
        core_arr, layer_input, gain_one, query_weight, key_weight, value_weight, extra
    )
    tops = digits[-1][1]
    staged = n_ctx == 8
    low, top = digits[0], digits[-1]
    turned_digits = digits[1:] + digits[:1]
    turned_keys = [(k[-1],) + k[:-1] for k in rel_keys(turned_digits)]
    owner_turned = jnp.stack(
        [digit_offset(me, k, digits, -1) for k in turned_keys]
    ).astype(jnp.int32)

    wo_chip = other_chip(output_weight)
    kv_weight = jnp.concatenate([key_weight, value_weight], axis=1)
    g_out = columns(owner_to, core_arr, cotangent, half, tops, [kv])
    if staged:
        z, y = [kv], []
        for r in range(tops - 1):
            aside = [g_out[0], kv_weight] if r == tops - 2 else []
            z_next, y_next = tie([hop(z[r], n_ctx, top), hop(z[r], n_ctx, low)], aside)
            z.append(z_next)
            y.append(y_next)
        y.append(hop(z[-1], n_ctx, low))
        kv_list = [block for pair in zip(z, y) for block in pair]
    else:
        kv_blocks = gather_ctx(kv, n_ctx, digits, upper_first)
        kv_list = [kv_blocks[k] for k in keys]

    g_top = exchange_top(g_out, n_ctx, digits)

    heads_f32, heads_near, heads_far, lse = attend(
        q, kv_list, heads, groups, first=[g_out[0]]
    )
    heads_near, heads_far, wo_chip, *rest = tie(
        [heads_near, heads_far, wo_chip] + list(g_top[1:]), []
    )
    g_top = [g_top[0]] + list(rest)
    wo_parts = [output_weight, other_core(output_weight), wo_chip, other_core(wo_chip)]

    parts = all_parts(heads_near, heads_far)
    g_pieces = exchange_rest(g_top, n_ctx, digits)
    hidden_one, a2_mine = simple(
        middle_kernel,
        "middle",
        [((half, width), F32), ((half, width), BF)],
        core_arr,
        layer_input,
        gain_two,
        *parts,
        *wo_parts,
    )
    a2_far = other_core(a2_mine)
    a2_out = columns(owner_to, core_arr, a2_mine, half, tops)
    a2_top = exchange_top(a2_out, n_ctx, digits)
    wq_chip = other_chip(query_weight)

    mix_keep, mix_send, dx_keep, dx_send, gates, ent = experts_call(
        core_arr,
        ids,
        a2_mine,
        a2_far,
        cotangent,
        router,
        gate_weight,
        up_weight,
        down_weight,
        first=[a2_out[0]],
    )
    dx_send, wq_chip, *rest = tie(
        [dx_send, wq_chip] + list(a2_top[1:]), [array for array, _ in g_pieces]
    )
    a2_top = [a2_top[0]] + list(rest)

    near = (dx_keep + other_core(dx_send).astype(F32)).astype(BF)
    got = other_chip(near)
    if staged:
        z_next, y_next = hop(ent, n_ctx, top), hop(ent, n_ctx, low)
        z, y = [ent], []
    hidden_grad, att_near, misc = simple(
        back_kernel,
        "back",
        [((half, width), F32), ((half, width), BF), ((16, width), F32)],
        core_arr,
        near,
        got,
        hidden_one,
        a2_mine,
        gates,
        ids,
        router,
        gain_two,
        cotangent,
    )
    att_far = other_core(att_near)
    (mix_send,) = tie([mix_send], [got])
    mix_near = (mix_keep + other_core(mix_send).astype(F32)).astype(BF)
    mix_got = other_chip(mix_near)
    wq_parts = [query_weight, other_core(query_weight), wq_chip, other_core(wq_chip)]
    a2_pieces = exchange_rest(a2_top, n_ctx, digits)
    if staged:
        z_next, y_next = tie([z_next, y_next], [att_near])
        z.append(z_next)
        y.append(y_next)
        z_next, y_next = hop(z[1], n_ctx, top), hop(z[1], n_ctx, low)

    begin = [att_near, att_far, output_weight, heads_f32]
    if staged:
        dkv_1, dkv_2, dkv_3, head_grad, delta, dq_going = attend_back(
            q,
            kv_list[0],
            lse,
            kv_list[2:8],
            heads,
            groups,
            start=begin,
            end=False,
            first=[z[1], y[0], mix_near],
        )
        z_next, y_next = tie([z_next, y_next], [dq_going])
        z.append(z_next)
        y.append(y_next)
        z_next, y_next = hop(z[2], n_ctx, top), hop(z[2], n_ctx, low)
        dkv_0, dq_near, dq_far = attend_back(
            q,
            kv_list[0],
            lse,
            kv_list[0:2],
            heads,
            groups,
            going=[head_grad, delta, dq_going],
            first=[z[2], y[1]] + [array for array, _ in a2_pieces],
        )
        dkv = [dkv_0, dkv_1, dkv_2, dkv_3]
    else:
        *dkv, head_grad, delta, dq_near, dq_far = attend_back(
            q, kv_list[0], lse, kv_list, heads, groups, start=begin
        )
        dkv = jnp.concatenate(dkv, axis=0)
    (mix_got,) = tie([mix_got], [dq_near])
    a2_stack, a2_stack_far = swapped(a2_pieces, [dq_near])
    g_stack, g_far = swapped(g_pieces, [dq_near])
    out_mine = hidden_one + mix_near.astype(F32) + mix_got.astype(F32)
    (layer_output,) = simple(
        place_kernel, "place", [((tok, width), F32)], core_arr, out_mine, other_core(out_mine)
    )

    terms = weight_terms(
        owner_from,
        [
            ([att_near, att_far], [heads_near, heads_far]),
            ([a1], [jnp.concatenate([dq_near, dq_far], axis=0)]),
        ],
        misc,
        6,
    )
    used = tok // (2 * kvw)
    ids_rows = jnp.stack(
        [b[tok + used : tok + 3 * used].astype(jnp.int32).reshape(2, tok) for b in kv_list], 0
    )
    ids_all = jnp.swapaxes(ids_rows, 1, 2)
    shared = [ids_all, a2_stack, a2_stack_far, g_stack, g_far]
    dq_parts = all_parts(dq_near, dq_far)
    (query_back,) = simple(
        query_back_kernel, "query_back", [((half, width), F32)], core_arr, *dq_parts, *wq_parts
    )
    if staged:
        sums = expert_grads(0, *shared, [z[0], y[0], z[1], y[1]], experts)
        z_next, y_next = tie([z_next, y_next], [sums[0]])
        z.append(z_next)
        y.append(y_next)
        waits = [[dq_near], [terms], [sums[0]], [query_back]]
        dkv_own = scatter_ctx(
            dkv, n_ctx, digits, add_bf, lambda at, x: tie([x], waits[at])[0]
        )
    else:
        dkv_own = scatter_ctx(dkv, n_ctx, digits, add_bf)

    (terms,) = tie([terms], [dkv_own])

    kv_chip = other_chip(kv_weight)
    (kv_chip,) = tie([kv_chip], [query_back])
    kv_weights = [kv_weight, other_core(kv_weight), kv_chip, other_core(kv_chip)]

    late = weight_terms(owner_turned, [([a1], [dkv_own])])
    dkv_parts = all_parts(dkv_own[:half], dkv_own[half:])
    in_mine, norm_row = simple(
        input_kernel,
        "input",
        [((half, width), F32), ((8, width), F32)],
        core_arr,
        layer_input,
        gain_one,
        hidden_grad,
        query_back,
        *dkv_parts,
        *kv_weights,
    )
    norm_rel = norm_row[0].reshape(n_ctx, cols)[owner_turned]
    in_far = other_core(in_mine)

    if staged:
        y.append(hop(tie([z[3]], [late])[0], n_ctx, low))
        sums = expert_grads(4, *shared, [z[2], y[2], z[3], y[3]], experts, sums)
        waits = [[late], [in_mine], [sums[0]], []]
        terms_own = scatter_ctx(
            terms, n_ctx, digits, add_bf, lambda at, x: tie([x], waits[at])[0]
        )
        waits = [[in_mine], [sums[0]], [], []]
        late_own = scatter_ctx(
            late, n_ctx, turned_digits, add_bf, lambda at, x: tie([x], waits[at])[0]
        )
    else:
        terms_own = scatter_ctx(terms, n_ctx, digits, add_bf)
        late_own = scatter_ctx(late, n_ctx, turned_digits, add_bf)
        ents = gather_ctx(ent, n_ctx, digits, upper_first)
        sums = None
        for at in range(0, n_ctx, 4):
            some = range(at, min(at + 4, n_ctx))
            sums = expert_grads(at, *shared, [ents[keys[i]] for i in some], experts, sums)
    (input_grad,) = simple(
        place_kernel, "place", [((tok, width), F32)], core_arr, in_mine, in_far
    )
    norm_own = scatter_ctx(norm_rel, n_ctx, turned_digits, jnp.add)
    terms_own = terms_own.astype(F32)
    late_own = late_own.astype(F32)
    down_grad, gate_grad, up_grad = sums
    down_grad = jnp.swapaxes(down_grad, 1, 2)

    qw = heads * HD
    output_grad = terms_own[:, :qw].T
    query_grad = terms_own[:, qw : 2 * qw]
    small = jnp.concatenate([terms_own[:, 2 * qw : 2 * qw + experts + 1], norm_own[:, None]], axis=1)
    small = small + other_core(small)
    return (
        layer_output,
        input_grad,
        small[:, experts + 1],
        query_grad,
        late_own[:, :kvw],
        late_own[:, kvw:],
        output_grad,
        small[:, experts],
        small[:, :experts],
        gate_grad,
        up_grad,
        down_grad,
    )


def solution(mesh):
    in_specs = (
        P("ctx", None),
        P("ctx"),
        P("ctx", None),
        P(),
        P(None, "wa"),
        P(None, "wa"),
        P(None, "wa"),
        P("wa", None),
        P(),
        P(),
        P(None, None, "wa"),
        P(None, None, "wa"),
        P(None, "wa", None),
        P("ctx", None),
    )
    out_specs = (
        P("ctx", None),
        P("ctx", None),
        P("ctx"),
        P("ctx", "wa"),
        P("ctx", "wa"),
        P("ctx", "wa"),
        P("wa", "ctx"),
        P("ctx"),
        P("ctx", None),
        P(None, "ctx", "wa"),
        P(None, "ctx", "wa"),
        P(None, "wa", "ctx"),
    )
    return jax.shard_map(
        functools.partial(per_device, mesh.shape["ctx"]),
        mesh=mesh,
        in_specs=in_specs,
        out_specs=out_specs,
        check_vma=False,
    )
```

time: 648 us -> 457 us (0.71)
  waiting for transfers between devices: 241 us -> 135 us
  local copies, waits for them, and re-layouts: 120 us -> 45.1 us
  Pallas kernels: 131 us -> 189 us
  other arithmetic: 59.1 us -> 21.1 us
  matrix products: 13.1 us -> 0 us
  starting transfers between devices: 72.8 us -> 60.3 us
    ppermute x45 -> x38, waiting for transfers between devices: 196 us -> 99.3 us  [hop(): return lax.ppermute(x, 'ctx', moved(n, digit, shift))]
    pallas_call x4 -> x47, Pallas kernels: 126 us -> 184 us  [the longest x2 39.6 us: attend_back(): pl.pallas_call(drop_first(kernel, len(operands), len(first)), out_shape=t...]
    unnamed x160 -> x137, local copies, waits for them, and re-layouts: 52.9 us -> 25.2 us
    another operation x36 -> x14, local copies, waits for them, and re-layouts: 26.8 us -> 2.21 us  [the longest x2 0.7 us: per_device(): jnp.stack([digit_offset(me, k, digits, -1) for k in turned_keys])]
    ppermute x45 -> x38, starting transfers between devices: 66.3 us -> 45.9 us  [hop(): return lax.ppermute(x, 'ctx', moved(n, digit, shift))]
    ppermute x4 -> x8, waiting for transfers between devices: 45.3 us -> 29.2 us  [other_chip(): return lax.ppermute(x, 'wa', [(i, i ^ 2) for i in range(4)])]
    dot_general x10 -> x0, matrix products: 13.1 us -> none  [the longest x1 3.55 us: per_device(): late = jnp.dot(a1_rel, rows, preferred_element_type=F32)]
    pallas_call x5 -> x0, local copies, waits for them, and re-layouts: 10.2 us -> none  [experts_call(): pl.pallas_call(experts_kernel, out_shape=(jax.ShapeDtypeStruct((half, wid...]
  transfers between devices with their start and end apart: 60 -> 67, of which waited for: 24 -> 26; matrix products, arithmetic and copies ran while one was open for 28% -> 8% of each run, Pallas kernels for 20% -> 39%
where the time goes in v2:
time: 457 us; the launch traced here: 452 us
  Pallas kernels  189 us (41%)
  waiting for transfers between devices  135 us (30%)
  starting transfers between devices  60.3 us (13%)
  local copies, waits for them, and re-layouts  45.1 us (10%)
  other arithmetic  21.1 us (5%)
    ppermute x38, waiting for transfers between devices, hop(): return lax.ppermute(x, 'ctx', moved(n, digit, shift))  99.3 us
    ppermute x38, starting transfers between devices, hop(): return lax.ppermute(x, 'ctx', moved(n, digit, shift))  45.9 us
    pallas_call x2, Pallas kernels, attend_back(): pl.pallas_call(drop_first(kernel, len(operands), len(first)), out_shape=t...  39.6 us
    pallas_call x1, Pallas kernels, experts_call(): pl.pallas_call(drop_first(experts_kernel, 9, len(first)), out_shape=(jax....  32.1 us
    pallas_call x6, Pallas kernels, simple(): pl.pallas_call(drop_first(kernel, 1 + len(operands), len(first)), out_sha...  31.2 us
    pallas_call x2, Pallas kernels, expert_grads(): pl.pallas_call(functools.partial(expert_grads_kernel, at, len(ents), prev...  30.4 us
    ppermute x8, waiting for transfers between devices, other_chip(): return lax.ppermute(x, 'wa', [(i, i ^ 2) for i in range(4)])  29.2 us
    pallas_call x1, Pallas kernels, attend(): pl.pallas_call(drop_first(functools.partial(attend_kernel, nb, heads, gro...  27.6 us
  transfers between devices with their start and end apart: 67, of which 26 were waited for; matrix products, arithmetic and copies ran while one was open for 8% of the time, Pallas kernels for 39%

profile of v2, /device:TPU:0, one launch (start us, length us, event | category | flops | bytes accessed | tf_op | source)
XLA Modules:
  0.0 452.0 jit_solution(4162324866867552047)
XLA Ops:
  4.0 5.0 %project.1 = (bf16[512,1536]{1,0:T(8,128)(2,1)}, bf16[512,384]{1,0:T(8,128)(2,1)}, bf16[528,256]{1,0:T(8,128)(2,1)}) custom-call(s32[1]{0:T(128)} %bitcast.core_ref.refs_0_, bf16[512,1536]{1,0:T(8,128)(2,1)} %x_ref.7, f32[1536]{0:T(1024)} %gain_ref.7, bf16[1536,384]{1,0:T(8,128)(2,1)} %refs_4_.5, bf16[1536,128]{1,0:T(8,128)(2,1)} %wk_ref.1, ...), custom_call_target="tpu_custom_call" | custom-call | flops 5000000000 | bytes 15000000 | tf_op jit(solution)/shard_map/project/pallas_call | solution.py:238
  13.5 7.2 %collective-permute-done.refs_0_ = bf16[528,256]{1,0:T(8,128)(2,1)S(1)} collective-permute-done((bf16[528,256]{1,0:T(8,128)(2,1)}, bf16[528,256]{1,0:T(8,128)(2,1)S(1)}, u32[]{:S(2)}, u32[]{:S(2)}) %collective-permute-start) | collective-permute-done | bytes 270368 | tf_op jit(solution)/shard_map/ppermute | solution.py:49
  25.4 6.3 %collective-permute-done.2.refs_0_ = bf16[528,256]{1,0:T(8,128)(2,1)S(1)} collective-permute-done((bf16[528,256]{1,0:T(8,128)(2,1)}, bf16[528,256]{1,0:T(8,128)(2,1)S(1)}, u32[]{:S(2)}, u32[]{:S(2)}) %collective-permute-start.2) | collective-permute-done | bytes 270368 | tf_op jit(solution)/shard_map/ppermute | solution.py:49
  50.2 27.6 %attend.1 = (f32[512,384]{1,0:T(8,128)}, bf16[256,384]{1,0:T(8,128)(2,1)}, bf16[256,384]{1,0:T(8,128)(2,1)}, f32[8,512]{1,0:T(8,128)}) custom-call(bf16[512,384]{1,0:T(8,128)(2,1)} %get-tuple-element.88.refs_0_, bf16[528,256]{1,0:T(8,128)(2,1)} %get-tuple-element.89.refs_0_.refs_1_.refs_3_, bf16[528,256]{1,0:T(8,128)(2,1)} %get-tuple-element.90.refs_2_.refs_4_, ...), custom_call_target="tpu_custom_call" | custom-call | flops 27000000512 | bytes 81000000 | tf_op jit(solution)/shard_map/attend/pallas_call | solution.py:337
  82.3 5.1 %collective-permute-done.12.refs_2_ = bf16[256,384]{1,0:T(8,128)(2,1)S(1)} collective-permute-done((bf16[256,384]{1,0:T(8,128)(2,1)}, bf16[256,384]{1,0:T(8,128)(2,1)S(1)}, u32[]{:S(2)}, u32[]{:S(2)}) %collective-permute-start.12) | collective-permute-done | bytes 196640 | tf_op jit(solution)/shard_map/ppermute | solution.py:57
  91.5 6.4 %middle.1 = (f32[256,1536]{1,0:T(8,128)}, bf16[256,1536]{1,0:T(8,128)(2,1)}) custom-call(s32[1]{0:T(128)} %bitcast.core_ref.refs_0_, bf16[512,1536]{1,0:T(8,128)(2,1)} %x_ref.7, f32[1536]{0:T(1024)} %gain_ref.6, bf16[256,384]{1,0:T(8,128)(2,1)} %get-tuple-element.102.refs_0_.refs_2_, bf16[256,384]{1,0:T(8,128)(2,1)} %copy-done.61, ...), custom_call_target="tpu_custom_call" | custom-call | flops 5000000000 | bytes 15000000 | tf_op jit(solution)/shard_map/middle/pallas_call | solution.py:707
  104.9 10.5 %collective-permute-start.19 = (bf16[2,192,256]{2,1,0:T(8,128)(2,1)}, bf16[2,192,256]{2,1,0:T(8,128)(2,1)S(1)}, u32[]{:S(2)}, u32[]{:S(2)}) collective-permute-start(bf16[2,192,256]{2,1,0:T(8,128)(2,1)} %get-tuple-element.113), channel_id=1, source_target_pairs={{0,16},{4,20},{8,24},{12,28},{16,0},{20,4},{24,8},{28,12},{1,17},{... | collective-permute-start | bytes 589832 | tf_op jit(solution)/shard_map/ppermute | solution.py:49
  118.5 32.1 %experts.1 = (f32[256,1536]{1,0:T(8,128)}, bf16[256,1536]{1,0:T(8,128)(2,1)}, f32[256,1664]{1,0:T(8,128)}, bf16[256,1664]{1,0:T(8,128)(2,1)}, f32[512,8]{1,0:T(8,128)}, /*index=5*/bf16[6,512,256]{2,1,0:T(8,128)(2,1)}) custom-call(s32[1]{0:T(128)} %bitcast.core_ref.refs_0_, s32[512,2]{1,0:T(8,128)} %get-tuple-element.191.refs_1_.ids_ref, ...), custom_call_target="tpu_custom_call" | custom-call | flops 32000000000 | bytes 96000000 | tf_op jit(solution)/shard_map/experts/pallas_call | solution.py:609
  155.6 20.5 %collective-permute-done.23.refs_1_.got_ref = bf16[256,1664]{1,0:T(8,128)(2,1)S(1)} collective-permute-done((bf16[256,1664]{1,0:T(8,128)(2,1)S(1)}, bf16[256,1664]{1,0:T(8,128)(2,1)S(1)}, u32[]{:S(2)}, u32[]{:S(2)}) %collective-permute-start.23) | collective-permute-done | bytes 852000 | tf_op jit(solution)/shard_map/ppermute | solution.py:57
  177.0 5.6 %back.1 = (f32[256,1536]{1,0:T(8,128)}, bf16[256,1536]{1,0:T(8,128)(2,1)}, f32[16,1536]{1,0:T(8,128)}) custom-call(s32[1]{0:T(128)} %bitcast.core_ref.refs_0_, bf16[256,1664]{1,0:T(8,128)(2,1)} %copy-done.30, bf16[256,1664]{1,0:T(8,128)(2,1)} %copy-done.29, f32[256,1536]{1,0:T(8,128)} %get-tuple-element.105.hidden_ref, ...), custom_call_target="tpu_custom_call" | custom-call | flops 5000000000 | bytes 15000000 | tf_op jit(solution)/shard_map/back/pallas_call | solution.py:707
  200.1 26.1 %attend_back.2 = (bf16[2,512,256]{2,1,0:T(8,128)(2,1)}, bf16[2,512,256]{2,1,0:T(8,128)(2,1)}, bf16[2,512,256]{2,1,0:T(8,128)(2,1)}, bf16[512,384]{1,0:T(8,128)(2...) custom-call(bf16[512,384]{1,0:T(8,128)(2,1)} %get-tuple-element.88.refs_0_, ...), custom_call_target="tpu_custom_call" | custom-call | flops 27000000512 | bytes 81000000 | tf_op jit(solution)/shard_map/attend_back/pallas_call | solution.py:483
  226.3 7.6 %collective-permute-done.29.refs_0_ = bf16[6,512,256]{2,1,0:T(8,128)(2,1)} collective-permute-done((bf16[6,512,256]{2,1,0:T(8,128)(2,1)}, bf16[6,512,256]{2,1,0:T(8,128)(2,1)}, u32[]{:S(2)}, u32[]{:S(2)}) %collective-permute-start.29) | collective-permute-done | bytes 1572896 | tf_op jit(solution)/shard_map/ppermute | solution.py:49
  233.9 5.2 %collective-permute-done.30.refs_1_ = bf16[6,512,256]{2,1,0:T(8,128)(2,1)S(1)} collective-permute-done((bf16[6,512,256]{2,1,0:T(8,128)(2,1)S(1)}, bf16[6,512,256]{2,1,0:T(8,128)(2,1)S(1)}, u32[]{:S(2)}, u32[]{:S(2)}) %collective-permute-start.30) | collective-permute-done | bytes 1572896 | tf_op jit(solution)/shard_map/ppermute | solution.py:49
  241.2 13.4 %attend_back.3 = (bf16[2,512,256]{2,1,0:T(8,128)(2,1)}, bf16[256,384]{1,0:T(8,128)(2,1)}, bf16[256,384]{1,0:T(8,128)(2,1)}) custom-call(bf16[512,384]{1,0:T(8,128)(2,1)} %get-tuple-element.88.refs_0_, bf16[528,256]{1,0:T(8,128)(2,1)} %get-tuple-element.89.refs_0_.refs_1_.refs_3_, f32[8,512]{1,0:T(8,128)} %get-tuple-element.119.refs_2_, ...), custom_call_target="tpu_custom_call" | custom-call | flops 8999999488 | bytes 27000000 | tf_op jit(solution)/shard_map/attend_back/pallas_call | solution.py:483
  263.4 6.1 %weight_terms.2.refs_1_.refs_0_ = bf16[8,192,896]{2,1,0:T(8,128)(2,1)} custom-call(s32[8]{0:T(128)} %stack.101.owner_ref, bf16[256,1536]{1,0:T(8,128)(2,1)} %get-tuple-element.121.refs_2_.refs_9_.refs_0_, bf16[256,1536]{1,0:T(8,128)(2,1)} %collective-permute-done.26.refs_10_.refs_1_, bf16[256,384]{1,0:T(8,128)(2,1)} %get-tuple-element.102.refs_0_.refs_2_, ...), custom_call_target="tpu_custom_call" | custom-call | flops 6000000000 | bytes 18000000 | tf_op jit(solution)/shard_map/weight_terms/pallas_call | solution.py:872
  270.3 5.6 %query_back.1.refs_1_.query_ref = f32[256,1536]{1,0:T(8,128)} custom-call(s32[1]{0:T(128)} %bitcast.core_ref.refs_0_, bf16[256,384]{1,0:T(8,128)(2,1)} %get-tuple-element.134.refs_1_.refs_0_.refs_5_, bf16[256,384]{1,0:T(8,128)(2,1)} %copy-done.58, bf16[256,384]{1,0:T(8,128)(2,1)} %copy-done.57, bf16[256,384]{1,0:T(8,128)(2,1)} %copy-done.60, ...), custom_call_target="tpu_custom_call" | custom-call | flops 5000000000 | bytes 15000000 | tf_op jit(solution)/shard_map/query_back/pallas_call | solution.py:707
  281.6 15.0 %expert_grads.2 = (f32[8,192,256]{2,1,0:T(8,128)}, f32[8,192,256]{2,1,0:T(8,128)}, f32[8,192,256]{2,1,0:T(8,128)}) custom-call(s32[8,512,2]{2,1,0:T(8,128)} %bitcast.53, bf16[8,192,256]{2,1,0:T(8,128)(2,1)} %stacked.6.refs_0_, bf16[8,192,256]{2,1,0:T(8,128)(2,1)} %collective-permute-done.41.refs_1_, bf16[8,192,256]{2,1,0:T(8,128)(2,1)} %stacked.7.refs_2_, ...), custom_call_target="tpu_custom_call" | custom-call | flops 14000000000 | bytes 42000000 | tf_op jit(solution)/shard_map/expert_grads/pallas_call | solution.py:689
  320.4 6.1 %input.1 = (f32[256,1536]{1,0:T(8,128)}, f32[8,1536]{1,0:T(8,128)}) custom-call(s32[1]{0:T(128)} %bitcast.core_ref.refs_0_, bf16[512,1536]{1,0:T(8,128)(2,1)} %x_ref.7, f32[1536]{0:T(1024)} %gain_ref.7, f32[256,1536]{1,0:T(8,128)} %get-tuple-element.135.grad_ref, f32[256,1536]{1,0:T(8,128)} %query_back.1.refs_1_.query_ref, bf16[256,256]{1,0:T(8,128)(2,1)} %copy-done.51, ...), custom_call_target="tpu_custom_call" | custom-call | flops 5000000000 | bytes 15000000 | tf_op jit(solution)/shard_map/input/pallas_call | solution.py:707
  334.2 7.5 %collective-permute-done.58 = f32[4,192]{1,0:T(4,128)S(1)} collective-permute-done((f32[4,192]{1,0:T(4,128)S(1)}, f32[4,192]{1,0:T(4,128)S(1)}, u32[]{:S(2)}, u32[]{:S(2)}) %collective-permute-start.58) | collective-permute-done | bytes 3104 | tf_op jit(solution)/shard_map/ppermute | solution.py:49
  353.9 4.5 collective-permute-done.60
  369.6 25.6 %collective-permute-done.63.refs_0_ = bf16[4,192,256]{2,1,0:T(8,128)(2,1)} collective-permute-done((bf16[4,192,256]{2,1,0:T(8,128)(2,1)}, bf16[4,192,256]{2,1,0:T(8,128)(2,1)}, u32[]{:S(2)}, u32[]{:S(2)}) %collective-permute-start.63) | collective-permute-done | bytes 393248 | tf_op jit(solution)/shard_map/ppermute | solution.py:49
  397.5 15.4 %expert_grads.3 = (f32[8,192,256]{2,1,0:T(8,128)}, f32[8,192,256]{2,1,0:T(8,128)}, f32[8,192,256]{2,1,0:T(8,128)}) custom-call(s32[8,512,2]{2,1,0:T(8,128)} %bitcast.54, bf16[8,192,256]{2,1,0:T(8,128)(2,1)} %stacked.6.refs_0_, bf16[8,192,256]{2,1,0:T(8,128)(2,1)} %collective-permute-done.41.refs_1_, bf16[8,192,256]{2,1,0:T(8,128)(2,1)} %stacked.7.refs_2_, ...), custom_call_target="tpu_custom_call" | custom-call | flops 14000000000 | bytes 42000000 | tf_op jit(solution)/shard_map/expert_grads/pallas_call | solution.py:689
  427.5 9.8 %collective-permute-done.66.refs_0_ = bf16[1,192,256]{2,1,0:T(8,128)(2,1)S(1)} collective-permute-done((bf16[1,192,256]{2,1,0:T(8,128)(2,1)S(1)}, bf16[1,192,256]{2,1,0:T(8,128)(2,1)S(1)}, u32[]{:S(2)}, u32[]{:S(2)}) %collective-permute-start.66) | collective-permute-done | bytes 98336 | tf_op jit(solution)/shard_map/ppermute | solution.py:49
  442.4 5.0 %collective-permute-done.57.refs_0_ = bf16[1,192,896]{2,1,0:T(8,128)(2,1)S(1)} collective-permute-done((bf16[1,192,896]{2,1,0:T(8,128)(2,1)S(1)}, bf16[1,192,896]{2,1,0:T(8,128)(2,1)S(1)}, u32[]{:S(2)}, u32[]{:S(2)}) %collective-permute-start.57) | collective-permute-done | bytes 344096 | tf_op jit(solution)/shard_map/ppermute | solution.py:49
  (369 shorter events, 171.2 us)
Async XLA Ops:
  43.8 34.0 %collective-permute-start.7 = (bf16[384,1536]{1,0:T(8,128)(2,1)}, bf16[384,1536]{1,0:T(8,128)(2,1)S(1)}, u32[]{:S(2)}, u32[]{:S(2)}) collective-permute-start(bf16[384,1536]{1,0:T(8,128)(2,1)} %refs_11_.1), channel_id=1, source_target_pairs={{0,2},{1,3},{2,0},{3,1},{4,6},{5,7},{6,4},{7,5},{8,10},{9,11},{10,... | collective-permute-start | bytes 3538952 | tf_op jit(solution)/shard_map/ppermute | solution.py:57
  45.3 35.6 %collective-permute-start.14 = (bf16[384,1536]{1,0:T(8,128)(2,1)}, bf16[384,1536]{1,0:T(8,128)(2,1)S(1)}, u32[]{:S(2)}, u32[]{:S(2)}) collective-permute-start(bf16[384,1536]{1,0:T(8,128)(2,1)} %refs_11_.1), channel_id=1, source_target_pairs={{0,1},{1,0},{2,3},{3,2},{4,5},{5,4},{6,7},{7,6},{8,9},{9,8},{10,11... | collective-permute-start | bytes 3538952 | tf_op jit(solution)/shard_map/ppermute | solution.py:53
  45.3 32.5 %collective-permute-start.10 = (bf16[2,192,256]{2,1,0:T(8,128)(2,1)}, bf16[2,192,256]{2,1,0:T(8,128)(2,1)S(1)}, u32[]{:S(2)}, u32[]{:S(2)}) collective-permute-start(bf16[2,192,256]{2,1,0:T(8,128)(2,1)} %get-tuple-element.101), channel_id=1, source_target_pairs={{0,24},{4,28},{8,0},{12,4},{16,8},{20,12},{24,16},{28,20},{1,25},{... | collective-permute-start | bytes 589832 | tf_op jit(solution)/shard_map/ppermute | solution.py:49
  98.6 52.0 %collective-permute-start.17 = (bf16[1536,384]{1,0:T(8,128)(2,1)}, bf16[1536,384]{1,0:T(8,128)(2,1)S(1)}, u32[]{:S(2)}, u32[]{:S(2)}) collective-permute-start(bf16[1536,384]{1,0:T(8,128)(2,1)} %refs_4_.5), channel_id=1, source_target_pairs={{0,2},{1,3},{2,0},{3,1},{4,6},{5,7},{6,4},{7,5},{8,10},{9,11},{10,... | collective-permute-start | bytes 3538952 | tf_op jit(solution)/shard_map/ppermute | solution.py:57
  101.7 49.0 %collective-permute-start.21 = (bf16[4,192,256]{2,1,0:T(8,128)(2,1)}, bf16[4,192,256]{2,1,0:T(8,128)(2,1)S(1)}, u32[]{:S(2)}, u32[]{:S(2)}) collective-permute-start(bf16[4,192,256]{2,1,0:T(8,128)(2,1)} %stacked.4), channel_id=1, source_target_pairs={{0,4},{4,0},{8,12},{12,8},{16,20},{20,16},{24,28},{28,24},{1,5},{5... | collective-permute-start | bytes 1179656 | tf_op jit(solution)/shard_map/ppermute | solution.py:49
  104.0 46.7 %collective-permute-start.18 = (bf16[2,192,256]{2,1,0:T(8,128)(2,1)}, bf16[2,192,256]{2,1,0:T(8,128)(2,1)S(1)}, u32[]{:S(2)}, u32[]{:S(2)}) collective-permute-start(bf16[2,192,256]{2,1,0:T(8,128)(2,1)} %get-tuple-element.112), channel_id=1, source_target_pairs={{0,8},{4,12},{8,16},{12,20},{16,24},{20,28},{24,0},{28,4},{1,9},{5... | collective-permute-start | bytes 589832 | tf_op jit(solution)/shard_map/ppermute | solution.py:49
  104.9 45.7 %collective-permute-start.19 = (bf16[2,192,256]{2,1,0:T(8,128)(2,1)}, bf16[2,192,256]{2,1,0:T(8,128)(2,1)S(1)}, u32[]{:S(2)}, u32[]{:S(2)}) collective-permute-start(bf16[2,192,256]{2,1,0:T(8,128)(2,1)} %get-tuple-element.113), channel_id=1, source_target_pairs={{0,16},{4,20},{8,24},{12,28},{16,0},{20,4},{24,8},{28,12},{1,17},{... | collective-permute-start | bytes 589832 | tf_op jit(solution)/shard_map/ppermute | solution.py:49
  115.4 35.3 %collective-permute-start.20 = (bf16[2,192,256]{2,1,0:T(8,128)(2,1)}, bf16[2,192,256]{2,1,0:T(8,128)(2,1)S(1)}, u32[]{:S(2)}, u32[]{:S(2)}) collective-permute-start(bf16[2,192,256]{2,1,0:T(8,128)(2,1)} %get-tuple-element.114), channel_id=1, source_target_pairs={{0,24},{4,28},{8,0},{12,4},{16,8},{20,12},{24,16},{28,20},{1,25},{... | collective-permute-start | bytes 589832 | tf_op jit(solution)/shard_map/ppermute | solution.py:49
  155.6 38.2 %collective-permute-start.27 = (bf16[6,512,256]{2,1,0:T(8,128)(2,1)}, bf16[6,512,256]{2,1,0:T(8,128)(2,1)S(1)}, u32[]{:S(2)}, u32[]{:S(2)}) collective-permute-start(bf16[6,512,256]{2,1,0:T(8,128)(2,1)} %get-tuple-element.123.refs_4_), channel_id=1, source_target_pairs={{0,8},{4,12},{8,16},{12,20},{16,24},{20,28},{24,0},{28,4},{1,9},{5... | collective-permute-start | bytes 4718600 | tf_op jit(solution)/shard_map/ppermute | solution.py:49
  155.6 39.7 %collective-permute-start.28 = (bf16[6,512,256]{2,1,0:T(8,128)(2,1)}, bf16[6,512,256]{2,1,0:T(8,128)(2,1)}, u32[]{:S(2)}, u32[]{:S(2)}) collective-permute-start(bf16[6,512,256]{2,1,0:T(8,128)(2,1)} %get-tuple-element.123.refs_4_), channel_id=1, source_target_pairs={{0,4},{4,0},{8,12},{12,8},{16,20},{20,16},{24,28},{28,24},{1,5},{5... | collective-permute-start | bytes 4718600 | tf_op jit(solution)/shard_map/ppermute | solution.py:49
  183.0 79.3 %collective-permute-start.36 = (bf16[1536,384]{1,0:T(8,128)(2,1)}, bf16[1536,384]{1,0:T(8,128)(2,1)}, u32[]{:S(2)}, u32[]{:S(2)}) collective-permute-start(bf16[1536,384]{1,0:T(8,128)(2,1)} %refs_4_.5), channel_id=1, source_target_pairs={{0,1},{1,0},{2,3},{3,2},{4,5},{5,4},{6,7},{7,6},{8,9},{9,8},{10,11... | collective-permute-start | bytes 3538952 | tf_op jit(solution)/shard_map/ppermute | solution.py:53
  193.8 82.1 %collective-permute-start.48 = (bf16[1536,256]{1,0:T(8,128)(2,1)}, bf16[1536,256]{1,0:T(8,128)(2,1)}, u32[]{:S(2)}, u32[]{:S(2)}) collective-permute-start(bf16[1536,256]{1,0:T(8,128)(2,1)} %constant_dynamic-update-slice_fusion.refs_3_.refs_4_), channel_id=1, source_target_pairs={{0,2},{1,3},{2,0},{3,1},{4,6},{5,7},{6,4},{7,5},{8,10},{9,11},{10,... | collective-permute-start | bytes 2359304 | tf_op jit(solution)/shard_map/ppermute | solution.py:57
  195.3 45.1 %collective-permute-start.31 = (bf16[4,192,256]{2,1,0:T(8,128)(2,1)}, bf16[4,192,256]{2,1,0:T(8,128)(2,1)S(1)}, u32[]{:S(2)}, u32[]{:S(2)}) collective-permute-start(bf16[4,192,256]{2,1,0:T(8,128)(2,1)} %stacked.5), channel_id=1, source_target_pairs={{0,4},{4,0},{8,12},{12,8},{16,20},{20,16},{24,28},{28,24},{1,5},{5... | collective-permute-start | bytes 1179656 | tf_op jit(solution)/shard_map/ppermute | solution.py:49
  195.3 38.5 %collective-permute-start.29 = (bf16[6,512,256]{2,1,0:T(8,128)(2,1)}, bf16[6,512,256]{2,1,0:T(8,128)(2,1)}, u32[]{:S(2)}, u32[]{:S(2)}) collective-permute-start(bf16[6,512,256]{2,1,0:T(8,128)(2,1)} %get-tuple-element.124.refs_13_.refs_6_), channel_id=1, source_target_pairs={{0,8},{4,12},{8,16},{12,20},{16,24},{20,28},{24,0},{28,4},{1,9},{5... | collective-permute-start | bytes 4718600 | tf_op jit(solution)/shard_map/ppermute | solution.py:49
  198.2 40.9 %collective-permute-start.30 = (bf16[6,512,256]{2,1,0:T(8,128)(2,1)S(1)}, bf16[6,512,256]{2,1,0:T(8,128)(2,1)S(1)}, u32[]{:S(2)}, u32[]{:S(2)}) collective-permute-start(bf16[6,512,256]{2,1,0:T(8,128)(2,1)S(1)} %copy-done.22), channel_id=1, source_target_pairs={{0,4},{4,0},{8,12},{12,8},{16,20},{20,16},{24,28},{28,24},{1,5},{5... | collective-permute-start | bytes 4718600 | tf_op jit(solution)/shard_map/ppermute | solution.py:49
  269.6 41.4 %collective-permute-start.47 = (bf16[1536,256]{1,0:T(8,128)(2,1)}, bf16[1536,256]{1,0:T(8,128)(2,1)}, u32[]{:S(2)}, u32[]{:S(2)}) collective-permute-start(bf16[1536,256]{1,0:T(8,128)(2,1)} %constant_dynamic-update-slice_fusion.refs_3_.refs_4_), channel_id=1, source_target_pairs={{0,1},{1,0},{2,3},{3,2},{4,5},{5,4},{6,7},{7,6},{8,9},{9,8},{10,11... | collective-permute-start | bytes 2359304 | tf_op jit(solution)/shard_map/ppermute | solution.py:53
  279.5 33.1 %collective-permute-start.49 = (bf16[1536,256]{1,0:T(8,128)(2,1)}, bf16[1536,256]{1,0:T(8,128)(2,1)}, u32[]{:S(2)}, u32[]{:S(2)}) collective-permute-start(bf16[1536,256]{1,0:T(8,128)(2,1)} %tie.42.refs_6_), channel_id=1, source_target_pairs={{0,1},{1,0},{2,3},{3,2},{4,5},{5,4},{6,7},{7,6},{8,9},{9,8},{10,11... | collective-permute-start | bytes 2359304 | tf_op jit(solution)/shard_map/ppermute | solution.py:53
  300.3 47.6 %collective-permute-start.54 = (bf16[6,512,256]{2,1,0:T(8,128)(2,1)}, bf16[6,512,256]{2,1,0:T(8,128)(2,1)S(1)}, u32[]{:S(2)}, u32[]{:S(2)}) collective-permute-start(bf16[6,512,256]{2,1,0:T(8,128)(2,1)} %get-tuple-element.129.refs_8_.refs_4_), channel_id=1, source_target_pairs={{0,8},{4,12},{8,16},{12,20},{16,24},{20,28},{24,0},{28,4},{1,9},{5... | collective-permute-start | bytes 4718600 | tf_op jit(solution)/shard_map/ppermute | solution.py:49
  303.2 44.7 %collective-permute-start.55 = (bf16[6,512,256]{2,1,0:T(8,128)(2,1)}, bf16[6,512,256]{2,1,0:T(8,128)(2,1)}, u32[]{:S(2)}, u32[]{:S(2)}) collective-permute-start(bf16[6,512,256]{2,1,0:T(8,128)(2,1)} %get-tuple-element.129.refs_8_.refs_4_), channel_id=1, source_target_pairs={{0,4},{4,0},{8,12},{12,8},{16,20},{20,16},{24,28},{28,24},{1,5},{5... | collective-permute-start | bytes 4718600 | tf_op jit(solution)/shard_map/ppermute | solution.py:49
  316.0 49.9 %collective-permute-start.32 = (f32[256,1536]{1,0:T(8,128)}, f32[256,1536]{1,0:T(8,128)}, u32[]{:S(2)}, u32[]{:S(2)}) collective-permute-start(f32[256,1536]{1,0:T(8,128)} %convert_add_fusion.mine_ref), channel_id=1, source_target_pairs={{0,1},{1,0},{2,3},{3,2},{4,5},{5,4},{6,7},{7,6},{8,9},{9,8},{10,11... | collective-permute-start | bytes 4718600 | tf_op jit(solution)/shard_map/ppermute | solution.py:53
  331.3 32.5 %collective-permute-start.51 = (bf16[2,192,896]{2,1,0:T(8,128)(2,1)}, bf16[2,192,896]{2,1,0:T(8,128)(2,1)}, u32[]{:S(2)}, u32[]{:S(2)}) collective-permute-start(bf16[2,192,896]{2,1,0:T(8,128)(2,1)} %slice.199), channel_id=1, source_target_pairs={{0,8},{4,12},{8,16},{12,20},{16,24},{20,28},{24,0},{28,4},{1,9},{5... | collective-permute-start | bytes 2064392 | tf_op jit(solution)/shard_map/ppermute | solution.py:49
  351.7 45.8 %collective-permute-start.56 = (bf16[6,512,256]{2,1,0:T(8,128)(2,1)}, bf16[6,512,256]{2,1,0:T(8,128)(2,1)}, u32[]{:S(2)}, u32[]{:S(2)}) collective-permute-start(bf16[6,512,256]{2,1,0:T(8,128)(2,1)} %tie.47), channel_id=1, source_target_pairs={{0,4},{4,0},{8,12},{12,8},{16,20},{20,16},{24,28},{28,24},{1,5},{5... | collective-permute-start | bytes 4718600 | tf_op jit(solution)/shard_map/ppermute | solution.py:49
  359.2 36.0 %collective-permute-start.63 = (bf16[4,192,256]{2,1,0:T(8,128)(2,1)}, bf16[4,192,256]{2,1,0:T(8,128)(2,1)}, u32[]{:S(2)}, u32[]{:S(2)}) collective-permute-start(bf16[4,192,256]{2,1,0:T(8,128)(2,1)} %slice.214), channel_id=1, source_target_pairs={{0,4},{4,0},{8,12},{12,8},{16,20},{20,16},{24,28},{28,24},{1,5},{5... | collective-permute-start | bytes 1179656 | tf_op jit(solution)/shard_map/ppermute | solution.py:49
  363.7 60.0 %collective-permute-start.50 = (f32[256,1536]{1,0:T(8,128)}, f32[256,1536]{1,0:T(8,128)}, u32[]{:S(2)}, u32[]{:S(2)}) collective-permute-start(f32[256,1536]{1,0:T(8,128)} %get-tuple-element.155.mine_ref.refs_1_), channel_id=1, source_target_pairs={{0,1},{1,0},{2,3},{3,2},{4,5},{5,4},{6,7},{7,6},{8,9},{9,8},{10,11... | collective-permute-start | bytes 4718600 | tf_op jit(solution)/shard_map/ppermute | solution.py:53
  (110 other events, 784.8 us)
